TPU v7x, 32 devices: a whole 2x2x4 slice. The times are simulated.
32 devices in a mesh: groups: 2 (over y), mp: 4 (over z), segment: 2 (over x), section: 2 (over core).
Axes of the slice: x: 2, y: 2, z: 4, core: 2. Of those that a mesh axis runs over, the one named last changes fastest.
Arguments:
- resp_rows: bfloat16 [32, 32, 4096], P(('groups', 'segment'), None, 'mp'), parts along dimension 0, may hold values from -6 to 6
- lengths: int32 [8, 4], P('groups'), parts along dimension 0, may hold values from 1 to 32, 64 in all within a row
- source: int32 [32], P('groups'), parts along dimension 0, may hold values from 0 to 15, each once
- w_query: bfloat16 [2, 2, 4096, 1024], P('section', 'segment', None, 'mp'), may hold values from -0.09375 to 0.09375
- w_keyval: bfloat16 [2, 2, 4096, 2, 128], P('section', 'segment', None, None, 'mp'), may hold values from -0.09375 to 0.09375
- w_out: bfloat16 [2, 2, 1024, 4096], P('section', 'segment', None, 'mp'), may hold values from -0.1875 to 0.1875
- gains: bfloat16 [2, 2, 4096], P('section', 'segment', 'mp'), may hold values from 0.25 to 1.75
- final_gain: bfloat16 [2, 4096], P('section', 'mp'), may hold values from 0.25 to 1.75
- head: bfloat16 [2, 4096], P('section', 'mp'), may hold values from -0.09375 to 0.09375
Outputs:
- hidden: bfloat16 [2, 8, 64, 4096], P('section', 'groups', 'segment', 'mp'), parts along dimension 1
- scores: float32 [2, 8, 64], P('section', 'groups'), parts along dimension 1
- advantage: float32 [32], P(('groups', 'section')), parts along dimension 0
There are 2 independent parts, one for each index of `groups`. A program takes and returns all parts, laid end to end along the dimension named above; an argument that names none is the same for every part. Nothing has to cross between parts.
Inputs may be any that keep to these rules, and one draw needn't show every extreme that they name: Each row of lengths sums to 64; its largest entry is exactly 32. source names every response once.
All inputs are finite; a program needn't handle non-finite values.
Results may differ from a plain program's by a relative error of at most 0.0085.
Values may be sent and summed in bfloat16 or wider, within the bound.
A program may use at most 64 MiB of HBM per device.

v0:
```python
import jax
import jax.numpy as jnp
from jax import lax
from jax.sharding import PartitionSpec as P

D = 4096
HEAD_DIM = 128
GROUP = 8
MB = 4
R_MB = 4
T_MB = 64
LMAX = 32
RESP = 16


epsilon = 1e-06
rope_base = 1000000.0


def shifted(block, axis, distance):
    devices = range(lax.axis_size(axis))
    route = [(i - distance, i) for i in devices if i - distance in devices]
    return lax.ppermute(block, axis, route)


def from_root(value, axis, root):
    mine = lax.axis_index(axis) == root
    return lax.psum(jnp.where(mine, value, jnp.zeros_like(value)), axis)


def from_partner(block, axis, stride):
    count = lax.axis_size(axis)
    route = []
    for low in range(count):
        high = low | 1 << stride
        if high != low and high < count:
            route += [(low, high), (high, low)]
    return lax.ppermute(block, axis, route)


def slot_tables(lengths, source):
    seg_ends = jnp.cumsum(lengths, axis=1)
    seg_starts = seg_ends - lengths
    places = jnp.arange(T_MB, dtype=jnp.int32)
    member = jnp.sum((places[None, :, None] >= seg_ends[:, None, :]).astype(jnp.int32), axis=2)
    one_hot = (member[:, :, None] == jnp.arange(R_MB, dtype=jnp.int32)[None, None, :]).astype(
        jnp.int32
    )
    position = places[None, :] - jnp.sum(one_hot * seg_starts[:, None, :], axis=2)
    owners = jnp.sum(one_hot * source.reshape(MB, R_MB)[:, None, :], axis=2)
    return (member, position, owners, seg_ends)


def angles(position):
    inv_freqs = rope_base ** (-jnp.arange(0, HEAD_DIM // 2, dtype=jnp.float32) * 2.0 / HEAD_DIM)
    phases = position.astype(jnp.float32)[..., None] * inv_freqs
    return (jnp.cos(phases), jnp.sin(phases))


def rotate(vectors, cosine, sine_part):
    half_dim = vectors.shape[-1] // 2
    first_half = vectors[..., :half_dim]
    second_half = vectors[..., half_dim:]
    return jnp.concatenate(
        [
            first_half * cosine - second_half * sine_part,
            second_half * cosine + first_half * sine_part,
        ],
        axis=-1,
    )


def segment_layer(
    tok_rows, member_row, cos_row, sin_row, norm_gain, query_w, keyval_w, output_w, head_ids
):
    tok_count = tok_rows.shape[0]
    rows_f32 = tok_rows.astype(jnp.float32)
    sq_sums = lax.psum(jnp.sum(rows_f32 * rows_f32, axis=1, keepdims=True), "mp")
    normed = (rows_f32 * lax.rsqrt(sq_sums / D + epsilon) * norm_gain.astype(jnp.float32)).astype(
        jnp.bfloat16
    )
    piece_rows = lax.all_gather(normed, "mp", axis=1, tiled=True)
    queries = jnp.dot(piece_rows, query_w, preferred_element_type=jnp.float32)
    keyval = jnp.dot(piece_rows, keyval_w, preferred_element_type=jnp.float32)
    cos_here = cos_row[:, None, :]
    sin_here = sin_row[:, None, :]
    queries = rotate(queries.reshape(tok_count, -1, HEAD_DIM), cos_here, sin_here).astype(
        jnp.bfloat16
    )
    local_keyval = keyval.astype(jnp.bfloat16).reshape(tok_count, 2, -1)
    all_keyval = lax.all_gather(local_keyval, "mp", axis=2, tiled=True)
    all_keyval = all_keyval.reshape(tok_count, 2, -1, HEAD_DIM)
    chosen = jnp.take(all_keyval, head_ids // GROUP, axis=2)
    key_rows = rotate(chosen[:, 0].astype(jnp.float32), cos_here, sin_here).astype(jnp.bfloat16)
    value_rows = chosen[:, 1]
    scores = jnp.einsum(
        "thd,shd->hts", queries, key_rows, preferred_element_type=jnp.float32
    ) * HEAD_DIM ** (-0.5)
    places = jnp.arange(tok_count, dtype=jnp.int32)
    visible = (member_row[:, None] == member_row[None, :]) & (places[None, :] <= places[:, None])
    scores = jnp.where(visible[None], scores, jnp.float32(-1e30))
    row_max = jnp.max(scores, axis=-1, keepdims=True)
    expo = jnp.exp(scores - row_max)
    weights = (expo / jnp.sum(expo, axis=-1, keepdims=True)).astype(jnp.bfloat16)
    attended = jnp.einsum(
        "hts,shd->thd", weights, value_rows, preferred_element_type=jnp.float32
    ).astype(jnp.bfloat16)
    attended = attended.reshape(tok_count, -1)
    projected = jnp.dot(
        lax.all_gather(attended, "mp", axis=1, tiled=True),
        output_w,
        preferred_element_type=jnp.float32,
    )
    return (rows_f32 + projected).astype(jnp.bfloat16)


def finish(final_rows, final_w, head_w):
    rows_f32 = final_rows.astype(jnp.float32)
    sq_sums = lax.psum(jnp.sum(rows_f32 * rows_f32, axis=-1, keepdims=True), "mp")
    normed = (rows_f32 * lax.rsqrt(sq_sums / D + epsilon) * final_w.astype(jnp.float32)).astype(
        jnp.bfloat16
    )
    partial_value = jnp.sum(normed.astype(jnp.float32) * head_w.astype(jnp.float32), axis=-1)
    scores = lax.psum(partial_value, "mp")
    return (normed, scores)


def per_device(resp_rows, lengths, source, w_query, w_keyval, w_out, gains, final_gain, head):
    segment_count = lax.axis_size("segment")
    segment_no = lax.axis_index("segment")
    mp_index = lax.axis_index("mp")
    member, position, owners, seg_ends = slot_tables(lengths, source)
    cosine, sine_part = angles(position)
    gathered = lax.all_gather(resp_rows, "segment", axis=0, tiled=True)
    local_width = gathered.shape[2]
    flat_pool = gathered.reshape(-1, local_width)
    packed = jnp.take(flat_pool, owners * LMAX + position, axis=0)
    query_w = w_query[0, 0]
    keyval_w = w_keyval[0, 0].reshape(D, -1)
    output_w = w_out[0, 0]
    norm_gain = gains[0, 0]
    heads_here = query_w.shape[1] // HEAD_DIM
    head_ids = mp_index * heads_here + jnp.arange(heads_here, dtype=jnp.int32)
    tick_count = MB + segment_count - 1

    def clock_step(tick_no, state_in):
        incoming, stored = state_in
        mb_index = tick_no - segment_no
        mb_slot = jnp.clip(mb_index, 0, MB - 1)
        first_in = lax.dynamic_index_in_dim(packed, jnp.clip(tick_no, 0, MB - 1), 0, keepdims=False)
        tok_rows = jnp.where(segment_no == 0, first_in, incoming)
        member_row = lax.dynamic_index_in_dim(member, mb_slot, 0, keepdims=False)
        cos_row = lax.dynamic_index_in_dim(cosine, mb_slot, 0, keepdims=False)
        sin_row = lax.dynamic_index_in_dim(sine_part, mb_slot, 0, keepdims=False)
        outcome = segment_layer(
            tok_rows, member_row, cos_row, sin_row, norm_gain, query_w, keyval_w, output_w, head_ids
        )
        keep_it = (segment_no == segment_count - 1) & (mb_index >= 0) & (mb_index < MB)
        current = lax.dynamic_index_in_dim(stored, mb_slot, 0, keepdims=False)
        stored = lax.dynamic_update_index_in_dim(
            stored, jnp.where(keep_it, outcome, current), mb_slot, 0
        )
        incoming = shifted(outcome, "segment", 1)
        return (incoming, stored)

    start_state = (
        jnp.zeros((T_MB, local_width), jnp.bfloat16),
        jnp.zeros((MB, T_MB, local_width), jnp.bfloat16),
    )
    incoming, stored = lax.fori_loop(0, tick_count, clock_step, start_state)
    rows_here = T_MB // segment_count
    final_rows = from_root(stored, "segment", segment_count - 1)
    normed_all, scores = finish(final_rows, final_gain[0], head[0])
    hidden = lax.dynamic_slice_in_dim(normed_all, segment_no * rows_here, rows_here, 1)[None]
    places = jnp.arange(T_MB, dtype=jnp.int32)
    last_pick = (places[None, None, :] == (seg_ends - 1)[:, :, None]).astype(jnp.float32)
    slot_scores = jnp.sum(last_pick * scores[:, None, :], axis=-1)
    other_side = from_partner(slot_scores, "section", 0)
    section_no = lax.axis_index("section")
    reward_val = jnp.where(section_no == 0, slot_scores, other_side)
    critic_val = jnp.where(section_no == 0, other_side, slot_scores)
    gap_slot = (reward_val - critic_val).reshape(-1)
    response_ids = jnp.arange(RESP, dtype=jnp.int32)
    matches = (source[None, :] == response_ids[:, None]).astype(jnp.float32)
    advantage = jnp.sum(matches * gap_slot[None, :], axis=1)
    half_count = RESP // 2
    own_part = lax.dynamic_slice_in_dim(advantage, section_no * half_count, half_count, 0)
    return (hidden, scores[None], own_part)


def solution(mesh):
    in_specs = (
        P(("groups", "segment"), None, "mp"),
        P("groups", None),
        P("groups"),
        P("section", "segment", None, "mp"),
        P("section", "segment", None, None, "mp"),
        P("section", "segment", None, "mp"),
        P("section", "segment", "mp"),
        P("section", "mp"),
        P("section", "mp"),
    )
    out_specs = (
        P("section", "groups", "segment", "mp"),
        P("section", "groups", None),
        P(("groups", "section")),
    )
    return jax.shard_map(
        per_device, mesh=mesh, in_specs=in_specs, out_specs=out_specs, check_vma=False
    )
```

profile of v0, /device:TPU:0, one launch (start us, length us, event | category | flops | bytes accessed | tf_op | source)
XLA Modules:
  0.0 424.3 jit_solution(15174630942692697623)
XLA Ops:
  14.2 19.4 %all-gather.2.cloned.1.call-done = bf16[16,32,1024]{2,1,0:T(8,128)(2,1)} async-done(((bf16[8,32,1024]{2,1,0:T(8,128)(2,1)}), bf16[16,32,1024]{2,1,0:T(8,128)(2,1)}) %all-gather.2.cloned.1.call-update) | async-done | bytes 1048592 | tf_op jit(solution)/shard_map/all_gather | solution.py:134
  37.8 326.0 %while.21 = (s32[]{:T(128)}, bf16[64,1024]{1,0:T(8,128)(2,1)S(1)}, bf16[4,64,1024]{2,1,0:T(8,128)(2,1)S(1)}, pred[]{:T(512)}, bf16[4,64,1024]{2,1,0:T(8,128)(2,1...) while((s32[]{:T(128)}, bf16[64,1024]{1,0:T(8,128)(2,1)S(1)}, ...), condition=%wide.region_9.10_spmd.clone.clone.clone, body=%wide.region_4.9_spmd.clone.clone.clone.sunk | while | flops 307365120 | bytes 9951303 | solution.py:170
  38.8 11.8 %psum.43 = f32[64,1]{0,1:T(1,128)S(1)} all-reduce(f32[64,1]{0,1:T(1,128)S(1)} %bitcast.105), channel_id=1, replica_groups=mesh['groups'=2,'mp'=4,'segment'=2,'section'=2] {'mp'}, use_global_device_ids=true, to_apply=%region_6.6 | all-reduce | flops 64 | bytes 512 | tf_op jit(solution)/shard_map/while/body/eval_jaxpr/psum | solution.py:78
  50.8 14.8 %all_gather.49 = bf16[64,4096]{1,0:T(8,128)(2,1)S(1)} all-gather(bf16[64,1024]{1,0:T(8,128)(2,1)S(1)} %fusion.84), channel_id=1, replica_groups=mesh['groups'=2,'mp'=4,'segment'=2,'section'=2] {'mp'}, dimensions={1}, use_global_device_ids=true | all-gather | bytes 655360 | tf_op jit(solution)/shard_map/while/body/eval_jaxpr/all_gather | solution.py:82
  67.2 13.3 %all_gather.50 = bf16[64,2,128]{0,2,1:T(8,128)(2,1)S(1)} all-gather(bf16[64,2,32]{0,2,1:T(8,128)(2,1)S(1)} %bitcast.101), channel_id=1, replica_groups=mesh['groups'=2,'mp'=4,'segment'=2,'section'=2] {'mp'}, dimensions={2}, use_global_device_ids=true | all-gather | bytes 40960 | tf_op jit(solution)/shard_map/while/body/eval_jaxpr/all_gather | solution.py:91
  82.8 13.3 %all_gather.51 = bf16[64,1024]{1,0:T(8,128)(2,1)S(1)} all-gather(bf16[64,256]{1,0:T(8,128)(2,1)S(1)} %bitcast.99), channel_id=1, replica_groups=mesh['groups'=2,'mp'=4,'segment'=2,'section'=2] {'mp'}, dimensions={1}, use_global_device_ids=true | all-gather | bytes 163840 | tf_op jit(solution)/shard_map/while/body/eval_jaxpr/all_gather | solution.py:110
  104.3 9.1 %psum.43 = f32[64,1]{0,1:T(1,128)S(1)} all-reduce(f32[64,1]{0,1:T(1,128)S(1)} %bitcast.105), channel_id=1, replica_groups=mesh['groups'=2,'mp'=4,'segment'=2,'section'=2] {'mp'}, use_global_device_ids=true, to_apply=%region_6.6 | all-reduce | flops 64 | bytes 512 | tf_op jit(solution)/shard_map/while/body/eval_jaxpr/psum | solution.py:78
  113.6 14.9 %all_gather.49 = bf16[64,4096]{1,0:T(8,128)(2,1)S(1)} all-gather(bf16[64,1024]{1,0:T(8,128)(2,1)S(1)} %fusion.84), channel_id=1, replica_groups=mesh['groups'=2,'mp'=4,'segment'=2,'section'=2] {'mp'}, dimensions={1}, use_global_device_ids=true | all-gather | bytes 655360 | tf_op jit(solution)/shard_map/while/body/eval_jaxpr/all_gather | solution.py:82
  130.0 13.1 %all_gather.50 = bf16[64,2,128]{0,2,1:T(8,128)(2,1)S(1)} all-gather(bf16[64,2,32]{0,2,1:T(8,128)(2,1)S(1)} %bitcast.101), channel_id=1, replica_groups=mesh['groups'=2,'mp'=4,'segment'=2,'section'=2] {'mp'}, dimensions={2}, use_global_device_ids=true | all-gather | bytes 40960 | tf_op jit(solution)/shard_map/while/body/eval_jaxpr/all_gather | solution.py:91
  145.5 13.4 %all_gather.51 = bf16[64,1024]{1,0:T(8,128)(2,1)S(1)} all-gather(bf16[64,256]{1,0:T(8,128)(2,1)S(1)} %bitcast.99), channel_id=1, replica_groups=mesh['groups'=2,'mp'=4,'segment'=2,'section'=2] {'mp'}, dimensions={1}, use_global_device_ids=true | all-gather | bytes 163840 | tf_op jit(solution)/shard_map/while/body/eval_jaxpr/all_gather | solution.py:110
  168.9 9.9 %psum.43 = f32[64,1]{0,1:T(1,128)S(1)} all-reduce(f32[64,1]{0,1:T(1,128)S(1)} %bitcast.105), channel_id=1, replica_groups=mesh['groups'=2,'mp'=4,'segment'=2,'section'=2] {'mp'}, use_global_device_ids=true, to_apply=%region_6.6 | all-reduce | flops 64 | bytes 512 | tf_op jit(solution)/shard_map/while/body/eval_jaxpr/psum | solution.py:78
  178.9 15.0 %all_gather.49 = bf16[64,4096]{1,0:T(8,128)(2,1)S(1)} all-gather(bf16[64,1024]{1,0:T(8,128)(2,1)S(1)} %fusion.84), channel_id=1, replica_groups=mesh['groups'=2,'mp'=4,'segment'=2,'section'=2] {'mp'}, dimensions={1}, use_global_device_ids=true | all-gather | bytes 655360 | tf_op jit(solution)/shard_map/while/body/eval_jaxpr/all_gather | solution.py:82
  195.6 13.2 %all_gather.50 = bf16[64,2,128]{0,2,1:T(8,128)(2,1)S(1)} all-gather(bf16[64,2,32]{0,2,1:T(8,128)(2,1)S(1)} %bitcast.101), channel_id=1, replica_groups=mesh['groups'=2,'mp'=4,'segment'=2,'section'=2] {'mp'}, dimensions={2}, use_global_device_ids=true | all-gather | bytes 40960 | tf_op jit(solution)/shard_map/while/body/eval_jaxpr/all_gather | solution.py:91
  211.1 13.7 %all_gather.51 = bf16[64,1024]{1,0:T(8,128)(2,1)S(1)} all-gather(bf16[64,256]{1,0:T(8,128)(2,1)S(1)} %bitcast.99), channel_id=1, replica_groups=mesh['groups'=2,'mp'=4,'segment'=2,'section'=2] {'mp'}, dimensions={1}, use_global_device_ids=true | all-gather | bytes 163840 | tf_op jit(solution)/shard_map/while/body/eval_jaxpr/all_gather | solution.py:110
  234.8 9.0 %psum.43 = f32[64,1]{0,1:T(1,128)S(1)} all-reduce(f32[64,1]{0,1:T(1,128)S(1)} %bitcast.105), channel_id=1, replica_groups=mesh['groups'=2,'mp'=4,'segment'=2,'section'=2] {'mp'}, use_global_device_ids=true, to_apply=%region_6.6 | all-reduce | flops 64 | bytes 512 | tf_op jit(solution)/shard_map/while/body/eval_jaxpr/psum | solution.py:78
  243.9 14.7 %all_gather.49 = bf16[64,4096]{1,0:T(8,128)(2,1)S(1)} all-gather(bf16[64,1024]{1,0:T(8,128)(2,1)S(1)} %fusion.84), channel_id=1, replica_groups=mesh['groups'=2,'mp'=4,'segment'=2,'section'=2] {'mp'}, dimensions={1}, use_global_device_ids=true | all-gather | bytes 655360 | tf_op jit(solution)/shard_map/while/body/eval_jaxpr/all_gather | solution.py:82
  260.2 13.4 %all_gather.50 = bf16[64,2,128]{0,2,1:T(8,128)(2,1)S(1)} all-gather(bf16[64,2,32]{0,2,1:T(8,128)(2,1)S(1)} %bitcast.101), channel_id=1, replica_groups=mesh['groups'=2,'mp'=4,'segment'=2,'section'=2] {'mp'}, dimensions={2}, use_global_device_ids=true | all-gather | bytes 40960 | tf_op jit(solution)/shard_map/while/body/eval_jaxpr/all_gather | solution.py:91
  275.9 13.3 %all_gather.51 = bf16[64,1024]{1,0:T(8,128)(2,1)S(1)} all-gather(bf16[64,256]{1,0:T(8,128)(2,1)S(1)} %bitcast.99), channel_id=1, replica_groups=mesh['groups'=2,'mp'=4,'segment'=2,'section'=2] {'mp'}, dimensions={1}, use_global_device_ids=true | all-gather | bytes 163840 | tf_op jit(solution)/shard_map/while/body/eval_jaxpr/all_gather | solution.py:110
  299.3 10.2 %psum.43 = f32[64,1]{0,1:T(1,128)S(1)} all-reduce(f32[64,1]{0,1:T(1,128)S(1)} %bitcast.105), channel_id=1, replica_groups=mesh['groups'=2,'mp'=4,'segment'=2,'section'=2] {'mp'}, use_global_device_ids=true, to_apply=%region_6.6 | all-reduce | flops 64 | bytes 512 | tf_op jit(solution)/shard_map/while/body/eval_jaxpr/psum | solution.py:78
  309.6 14.7 %all_gather.49 = bf16[64,4096]{1,0:T(8,128)(2,1)S(1)} all-gather(bf16[64,1024]{1,0:T(8,128)(2,1)S(1)} %fusion.84), channel_id=1, replica_groups=mesh['groups'=2,'mp'=4,'segment'=2,'section'=2] {'mp'}, dimensions={1}, use_global_device_ids=true | all-gather | bytes 655360 | tf_op jit(solution)/shard_map/while/body/eval_jaxpr/all_gather | solution.py:82
  326.0 13.1 %all_gather.50 = bf16[64,2,128]{0,2,1:T(8,128)(2,1)S(1)} all-gather(bf16[64,2,32]{0,2,1:T(8,128)(2,1)S(1)} %bitcast.101), channel_id=1, replica_groups=mesh['groups'=2,'mp'=4,'segment'=2,'section'=2] {'mp'}, dimensions={2}, use_global_device_ids=true | all-gather | bytes 40960 | tf_op jit(solution)/shard_map/while/body/eval_jaxpr/all_gather | solution.py:91
  341.4 13.3 %all_gather.51 = bf16[64,1024]{1,0:T(8,128)(2,1)S(1)} all-gather(bf16[64,256]{1,0:T(8,128)(2,1)S(1)} %bitcast.99), channel_id=1, replica_groups=mesh['groups'=2,'mp'=4,'segment'=2,'section'=2] {'mp'}, dimensions={1}, use_global_device_ids=true | all-gather | bytes 163840 | tf_op jit(solution)/shard_map/while/body/eval_jaxpr/all_gather | solution.py:110
  364.7 28.0 %all-reduce.2.cloned.1.call-done = bf16[4,64,1024]{2,1,0:T(8,128)(2,1)} async-done(((bf16[4,64,1024]{2,1,0:T(8,128)(2,1)}), bf16[4,64,1024]{2,1,0:T(8,128)(2,1)}) %all-reduce.2.cloned.1.call-update) | async-done | bytes 524304 | tf_op jit(solution)/shard_map/psum | solution.py:28
  393.9 11.7 %psum.37 = f32[4,64,1]{1,0,2:T(4,128)S(1)} all-reduce(f32[4,64,1]{1,0,2:T(4,128)S(1)} %bitcast.106), channel_id=1, replica_groups=mesh['groups'=2,'mp'=4,'segment'=2,'section'=2] {'mp'}, use_global_device_ids=true, to_apply=%region_12.13 | all-reduce | flops 256 | bytes 2048 | tf_op jit(solution)/shard_map/psum | solution.py:119
  (169 shorter events, 93.1 us)
Async XLA Ops:
  7.2 5.7 %copy-start.4 = (bf16[1,1,1024]{2,1,0:T(2,128)(2,1)S(1)}, bf16[1,1,1024]{2,1,0:T(2,128)(2,1)}, u32[]{:S(2)}) copy-start(bf16[1,1,1024]{2,1,0:T(2,128)(2,1)} %param.17) | copy-start | bytes 6148
  7.2 26.5 %all-gather.2.cloned.1.call-start = ((), (), s32[]{:S(2)}) async-start(), calls=%async_computation | async-start | bytes 1572864 | tf_op jit(solution)/shard_map/all_gather | solution.py:134
  7.9 384.8 %all-reduce.2.cloned.1.call-start = ((), (), s32[]{:S(2)}) async-start(), calls=%async_computation.1 | async-start | bytes 1048576 | tf_op jit(solution)/shard_map/psum | solution.py:28
  33.6 4.1 copy-start
  37.7 326.9 %copy-start.2 = (bf16[1,1024]{1,0:T(2,128)(2,1)S(1)}, bf16[1,1024]{1,0:T(2,128)(2,1)}, u32[]{:S(2)}) copy-start(bf16[1,1024]{1,0:T(2,128)(2,1)} %param.19) | copy-start | bytes 6148
  37.7 326.9 %copy-start.3 = (bf16[1,1024]{1,0:T(2,128)(2,1)S(1)}, bf16[1,1024]{1,0:T(2,128)(2,1)}, u32[]{:S(2)}) copy-start(bf16[1,1024]{1,0:T(2,128)(2,1)} %param.18) | copy-start | bytes 6148
  98.3 5.0 %collective-permute-start = (bf16[64,1024]{1,0:T(8,128)(2,1)S(1)}, bf16[64,1024]{1,0:T(8,128)(2,1)S(1)}, u32[]{:S(2)}, u32[]{:S(2)}) collective-permute-start(bf16[64,1024]{1,0:T(8,128)(2,1)S(1)} %get-tuple-element.723), channel_id=1, source_target_pairs={{0,2},{1,3},{4,6},{5,7},{8,10},{9,11},{12,14},{13,15},{16,18},{17,... | collective-permute-start | bytes 393224 | tf_op jit(solution)/shard_map/while/body/eval_jaxpr/ppermute | solution.py:23
  161.0 6.8 %collective-permute-start = (bf16[64,1024]{1,0:T(8,128)(2,1)S(1)}, bf16[64,1024]{1,0:T(8,128)(2,1)S(1)}, u32[]{:S(2)}, u32[]{:S(2)}) collective-permute-start(bf16[64,1024]{1,0:T(8,128)(2,1)S(1)} %get-tuple-element.723), channel_id=1, source_target_pairs={{0,2},{1,3},{4,6},{5,7},{8,10},{9,11},{12,14},{13,15},{16,18},{17,... | collective-permute-start | bytes 393224 | tf_op jit(solution)/shard_map/while/body/eval_jaxpr/ppermute | solution.py:23
  226.9 6.9 %collective-permute-start = (bf16[64,1024]{1,0:T(8,128)(2,1)S(1)}, bf16[64,1024]{1,0:T(8,128)(2,1)S(1)}, u32[]{:S(2)}, u32[]{:S(2)}) collective-permute-start(bf16[64,1024]{1,0:T(8,128)(2,1)S(1)} %get-tuple-element.723), channel_id=1, source_target_pairs={{0,2},{1,3},{4,6},{5,7},{8,10},{9,11},{12,14},{13,15},{16,18},{17,... | collective-permute-start | bytes 393224 | tf_op jit(solution)/shard_map/while/body/eval_jaxpr/ppermute | solution.py:23
  291.4 6.9 %collective-permute-start = (bf16[64,1024]{1,0:T(8,128)(2,1)S(1)}, bf16[64,1024]{1,0:T(8,128)(2,1)S(1)}, u32[]{:S(2)}, u32[]{:S(2)}) collective-permute-start(bf16[64,1024]{1,0:T(8,128)(2,1)S(1)} %get-tuple-element.723), channel_id=1, source_target_pairs={{0,2},{1,3},{4,6},{5,7},{8,10},{9,11},{12,14},{13,15},{16,18},{17,... | collective-permute-start | bytes 393224 | tf_op jit(solution)/shard_map/while/body/eval_jaxpr/ppermute | solution.py:23
  356.9 6.9 %collective-permute-start = (bf16[64,1024]{1,0:T(8,128)(2,1)S(1)}, bf16[64,1024]{1,0:T(8,128)(2,1)S(1)}, u32[]{:S(2)}, u32[]{:S(2)}) collective-permute-start(bf16[64,1024]{1,0:T(8,128)(2,1)S(1)} %get-tuple-element.723), channel_id=1, source_target_pairs={{0,2},{1,3},{4,6},{5,7},{8,10},{9,11},{12,14},{13,15},{16,18},{17,... | collective-permute-start | bytes 393224 | tf_op jit(solution)/shard_map/while/body/eval_jaxpr/ppermute | solution.py:23
  363.8 53.0 %copy-start.5 = (s32[16]{0:T(128)S(1)}, s32[16]{0:T(128)}, u32[]{:S(2)}) copy-start(s32[16]{0:T(128)} %param.13) | copy-start | bytes 196
  415.4 2.1 copy-start.1
  415.5 1.2 collective-permute-start.1
Sparse Core Ops, SparseCore 0:
  9.6 24.0 all-gather.1
  364.7 27.8 all-reduce.1
where the time goes:
time: 426 us; the launch traced here: 424 us
  blocking collectives  277 us (65%)
  waiting for transfers between devices  61 us (14%)
  matrix products  22.8 us (5%)
  starting transfers between devices  19.9 us (5%)
  other arithmetic  14.9 us (3%)
  between operations  14.2 us (3%)
  local copies, waits for them, and re-layouts  13.6 us (3%)
    all_gather x5, blocking collectives, segment_layer(): piece_rows = lax.all_gather(normed, 'mp', axis=1, tiled=True)  74.1 us
    all_gather x5, blocking collectives, segment_layer(): lax.all_gather(attended, 'mp', axis=1, tiled=True)  67.1 us
    all_gather x5, blocking collectives, segment_layer(): all_keyval = lax.all_gather(local_keyval, 'mp', axis=2, tiled=True)  66.1 us
    psum x5, blocking collectives, segment_layer(): lax.psum(jnp.sum(rows_f32 * rows_f32, axis=1, keepdims=True), 'mp')  50.1 us
    psum x1, waiting for transfers between devices, from_root(): return lax.psum(jnp.where(mine, value, jnp.zeros_like(value)), axis)  28 us
    ppermute x5, starting transfers between devices, shifted(): return lax.ppermute(block, axis, route)  19.9 us
    all_gather x1, waiting for transfers between devices, per_device(): gathered = lax.all_gather(resp_rows, 'segment', axis=0, tiled=True)  19.4 us
    ppermute x5, waiting for transfers between devices, shifted(): return lax.ppermute(block, axis, route)  12.5 us
  transfers between devices with their start and end apart: 8, of which 8 were waited for; matrix products, arithmetic and copies ran while one was open for 2% of the time, Pallas kernels for 0%

commit v1 on v0

v1 whole, which is shorter than its diff:
```python
import jax
import jax.numpy as jnp
from jax import lax
from jax.sharding import PartitionSpec as P

D = 4096
HEAD_DIM = 128
GROUP = 8
MB = 4
R_MB = 4
T_MB = 64
LMAX = 32
RESP = 16


epsilon = 1e-06
rope_base = 1000000.0


def from_partner(block, axis, stride):
    count = lax.axis_size(axis)
    route = []
    for low in range(count):
        high = low | 1 << stride
        if high != low and high < count:
            route += [(low, high), (high, low)]
    return lax.ppermute(block, axis, route)


def slot_tables(lengths, source):
    seg_ends = jnp.cumsum(lengths, axis=1)
    seg_starts = seg_ends - lengths
    places = jnp.arange(T_MB, dtype=jnp.int32)
    member = jnp.sum((places[None, :, None] >= seg_ends[:, None, :]).astype(jnp.int32), axis=2)
    one_hot = (member[:, :, None] == jnp.arange(R_MB, dtype=jnp.int32)[None, None, :]).astype(
        jnp.int32
    )
    position = places[None, :] - jnp.sum(one_hot * seg_starts[:, None, :], axis=2)
    owners = jnp.sum(one_hot * source.reshape(MB, R_MB)[:, None, :], axis=2)
    return (member, position, owners, seg_ends)


def angles(position):
    inv_freqs = rope_base ** (-jnp.arange(0, HEAD_DIM // 2, dtype=jnp.float32) * 2.0 / HEAD_DIM)
    phases = position.astype(jnp.float32)[..., None] * inv_freqs
    return (jnp.cos(phases), jnp.sin(phases))


def rotate(vectors, cosine, sine_part):
    half_dim = vectors.shape[-1] // 2
    first_half = vectors[..., :half_dim]
    second_half = vectors[..., half_dim:]
    return jnp.concatenate(
        [
            first_half * cosine - second_half * sine_part,
            second_half * cosine + first_half * sine_part,
        ],
        axis=-1,
    )


def layer(tok_rows, visible, cosine, sine_part, gain_all, query_w, keyval_w, output_w):
    width = tok_rows.shape[1]
    whole = lax.all_gather(tok_rows, "mp", axis=1, tiled=True)
    rows_f32 = whole.astype(jnp.float32)
    sq_sums = jnp.sum(rows_f32 * rows_f32, axis=1, keepdims=True)
    normed = (rows_f32 * lax.rsqrt(sq_sums / D + epsilon) * gain_all).astype(jnp.bfloat16)
    keyval = jnp.dot(normed, keyval_w, preferred_element_type=jnp.float32).astype(jnp.bfloat16)
    queries = jnp.dot(normed, query_w, preferred_element_type=jnp.float32)
    heads_here = query_w.shape[1] // HEAD_DIM
    kv_width = keyval_w.shape[1] // 2
    per_head = HEAD_DIM // kv_width
    all_keyval = lax.all_gather(keyval.reshape(MB, T_MB, 2, kv_width), "mp", axis=0)
    head_no = lax.axis_index("mp") * heads_here // GROUP
    chosen = lax.dynamic_slice_in_dim(all_keyval, head_no * per_head, per_head, 0)
    chosen = jnp.moveaxis(chosen, 0, 3).reshape(MB, T_MB, 2, HEAD_DIM)
    key_rows = rotate(chosen[:, :, 0].astype(jnp.float32), cosine, sine_part).astype(jnp.bfloat16)
    value_rows = chosen[:, :, 1]
    queries = rotate(
        queries.reshape(MB, T_MB, -1, HEAD_DIM), cosine[:, :, None, :], sine_part[:, :, None, :]
    ).astype(jnp.bfloat16)
    scores = jnp.einsum(
        "bthd,bsd->bhts", queries, key_rows, preferred_element_type=jnp.float32
    ) * HEAD_DIM ** (-0.5)
    scores = jnp.where(visible[:, None], scores, jnp.float32(-1e30))
    row_max = jnp.max(scores, axis=-1, keepdims=True)
    expo = jnp.exp(scores - row_max)
    weights = (expo / jnp.sum(expo, axis=-1, keepdims=True)).astype(jnp.bfloat16)
    attended = jnp.einsum(
        "bhts,bsd->bthd", weights, value_rows, preferred_element_type=jnp.float32
    ).astype(jnp.bfloat16)
    attended = attended.reshape(MB * T_MB, -1)
    projected = jnp.dot(
        lax.all_gather(attended, "mp", axis=1, tiled=True),
        output_w,
        preferred_element_type=jnp.float32,
    )
    return (tok_rows.astype(jnp.float32) + projected).astype(jnp.bfloat16)


def per_device(resp_rows, lengths, source, w_query, w_keyval, w_out, gains, final_gain, head):
    segment_count = lax.axis_size("segment")
    segment_no = lax.axis_index("segment")
    member, position, owners, seg_ends = slot_tables(lengths, source)
    cosine, sine_part = angles(position)
    places = jnp.arange(T_MB, dtype=jnp.int32)
    visible = (member[:, :, None] == member[:, None, :]) & (
        places[None, None, :] <= places[None, :, None]
    )
    gathered = lax.all_gather(resp_rows, "segment", axis=0, tiled=True)
    width = gathered.shape[2]
    x = jnp.take(gathered.reshape(-1, width), (owners * LMAX + position).reshape(-1), axis=0)
    gain_all = lax.all_gather(gains[0, 0], "mp", axis=0, tiled=True).astype(jnp.float32)
    query_w = w_query[0, 0]
    keyval_w = w_keyval[0, 0].reshape(D, -1)
    output_w = w_out[0, 0]
    for step in range(segment_count):
        y = layer(x, visible, cosine, sine_part, gain_all, query_w, keyval_w, output_w)
        if step < segment_count - 1:
            x = lax.ppermute(y, "segment", [(step, step + 1)])
    last = segment_count - 1
    rows_here = T_MB // segment_count
    y = y.reshape(MB, T_MB, width)
    blocks = [y[:, i * rows_here : (i + 1) * rows_here] for i in range(segment_count)]
    mine = blocks[last]
    for i in range(last):
        came = lax.ppermute(blocks[i], "segment", [(last, i)])
        mine = jnp.where(segment_no == i, came, mine)
    rows_f32 = mine.astype(jnp.float32)
    lift = final_gain[0].astype(jnp.float32)
    sums = jnp.stack(
        [jnp.sum(rows_f32 * rows_f32, axis=-1), jnp.sum(rows_f32 * (lift * head[0].astype(jnp.float32)), axis=-1)]
    )
    sums = jnp.sum(lax.all_gather(sums, "mp", axis=0), axis=0)
    scale = lax.rsqrt(sums[0] / D + epsilon)
    hidden = (rows_f32 * scale[..., None] * lift).astype(jnp.bfloat16)[None]
    scores = lax.all_gather(sums[1] * scale, "segment", axis=1, tiled=True)
    last_pick = (places[None, None, :] == (seg_ends - 1)[:, :, None]).astype(jnp.float32)
    slot_scores = jnp.sum(last_pick * scores[:, None, :], axis=-1)
    other_side = from_partner(slot_scores, "section", 0)
    section_no = lax.axis_index("section")
    gap_slot = jnp.where(section_no == 0, slot_scores - other_side, other_side - slot_scores).reshape(-1)
    half_count = RESP // 2
    response_ids = section_no * half_count + jnp.arange(half_count, dtype=jnp.int32)
    matches = (source[None, :] == response_ids[:, None]).astype(jnp.float32)
    own_part = jnp.sum(matches * gap_slot[None, :], axis=1)
    return (hidden, scores[None], own_part)


def solution(mesh):
    in_specs = (
        P(("groups", "segment"), None, "mp"),
        P("groups", None),
        P("groups"),
        P("section", "segment", None, "mp"),
        P("section", "segment", None, None, "mp"),
        P("section", "segment", None, "mp"),
        P("section", "segment", "mp"),
        P("section", "mp"),
        P("section", "mp"),
    )
    out_specs = (
        P("section", "groups", "segment", "mp"),
        P("section", "groups", None),
        P(("groups", "section")),
    )
    return jax.shard_map(
        per_device, mesh=mesh, in_specs=in_specs, out_specs=out_specs, check_vma=False
    )
```

time: 426 us -> 259 us (0.61)
  blocking collectives: 277 us -> 88.6 us
  waiting for transfers between devices: 61 us -> 111 us
  starting transfers between devices: 19.9 us -> 4.81 us
  matrix products: 22.8 us -> 12.8 us
    all_gather x15 -> x7, blocking collectives: 207 us -> 88.6 us  [the longest x2 29.4 us: layer(): lax.all_gather(attended, 'mp', axis=1, tiled=True)]
    all_gather x0 -> x2, waiting for transfers between devices: none -> 74.4 us  [layer(): whole = lax.all_gather(tok_rows, 'mp', axis=1, tiled=True)]
    psum x7 -> x0, blocking collectives: 70.1 us -> none  [the longest x5 50.1 us: segment_layer(): lax.psum(jnp.sum(rows_f32 * rows_f32, axis=1, keepdims=True), 'mp')]
    psum x1 -> x0, waiting for transfers between devices: 28 us -> none  [from_root(): return lax.psum(jnp.where(mine, value, jnp.zeros_like(value)), axis)]
    ppermute x5 -> x2, starting transfers between devices: 19.9 us -> 4.69 us  [the longest x1 3.4 us: per_device(): x = lax.ppermute(y, 'segment', [(step, step + 1)])]
    dot_general x20 -> x10, matrix products: 21.5 us -> 9.64 us  [the longest x2 3.7 us: layer(): queries = jnp.dot(normed, query_w, preferred_element_type=jnp.float32)]
    ppermute x5 -> x2, waiting for transfers between devices: 12.5 us -> 13.5 us  [the longest x1 6.88 us: per_device(): came = lax.ppermute(blocks[i], 'segment', [(last, i)])]
  transfers between devices with their start and end apart: 8 -> 6, of which waited for: 8 -> 6; matrix products, arithmetic and copies ran while one was open for 2% -> 3% of each run, Pallas kernels for 0% -> 0%
where the time goes in v1:
time: 259 us
  waiting for transfers between devices  111 us (43%)
  blocking collectives  88.6 us (34%)
  between operations  14.3 us (6%)
  local copies, waits for them, and re-layouts  13.9 us (5%)
  other arithmetic  13.2 us (5%)
  matrix products  12.8 us (5%)
  starting transfers between devices  4.81 us (2%)
    all_gather x2, waiting for transfers between devices, layer(): whole = lax.all_gather(tok_rows, 'mp', axis=1, tiled=True)  74.4 us
    all_gather x2, blocking collectives, layer(): lax.all_gather(attended, 'mp', axis=1, tiled=True)  29.4 us
    all_gather x2, blocking collectives, layer(): lax.all_gather(keyval.reshape(MB, T_MB, 2, kv_width), 'mp', axis=0)  28.4 us
    all_gather x1, waiting for transfers between devices, per_device(): gathered = lax.all_gather(resp_rows, 'segment', axis=0, tiled=True)  22.4 us
    all_gather x1, blocking collectives, per_device(): lax.all_gather(gains[0, 0], 'mp', axis=0, tiled=True).astype(jnp.float32)  13.3 us
    all_gather x1, blocking collectives, per_device(): sums = jnp.sum(lax.all_gather(sums, 'mp', axis=0), axis=0)  13.1 us
    ppermute x1, waiting for transfers between devices, per_device(): came = lax.ppermute(blocks[i], 'segment', [(last, i)])  6.88 us
    ppermute x1, waiting for transfers between devices, per_device(): x = lax.ppermute(y, 'segment', [(step, step + 1)])  6.65 us
  transfers between devices with their start and end apart: 6, of which 6 were waited for; matrix products, arithmetic and copies ran while one was open for 3% of the time, Pallas kernels for 0%

profile of v1, /device:TPU:0, one launch (start us, length us, event | category | flops | bytes accessed | tf_op | source)
XLA Modules:
  0.0 258.8 jit_solution(16574704889292380213)
XLA Ops:
  8.8 1.3 broadcast_add_fusion
  11.2 22.4 %all-gather.7.cloned.1.call-done = bf16[16,32,1024]{2,1,0:T(8,128)(2,1)} async-done(((bf16[8,32,1024]{2,1,0:T(8,128)(2,1)}), bf16[16,32,1024]{2,1,0:T(8,128)(2,1)}) %all-gather.7.cloned.1.call-update) | async-done | bytes 1048592 | tf_op jit(solution)/shard_map/all_gather | solution.py:110
  33.6 2.9 %gather_fusion = bf16[256,1024]{1,0:T(8,128)(2,1)S(1)} fusion(bf16[512,1024]{1,0:T(8,128)(2,1)} %bitcast.153, s32[1024]{0:T(1024)S(1)} %pad_clamp_fusion), kind=kCustom, calls=%fused_computation | custom fusion | bytes 1049600 | tf_op jit(solution)/shard_map/jit(_take)/gather | solution.py:112
  37.5 13.3 %all-gather = bf16[1,1,4096]{2,1,0:T(2,128)(2,1)S(1)} all-gather(bf16[1,1,1024]{2,1,0:T(2,128)(2,1)S(1)} %copy-done.20), channel_id=2, replica_groups=mesh['groups'=2,'mp'=4,'segment'=2,'section'=2] {'mp'}, dimensions={2}, use_global_device_ids=true | all-gather | bytes 10240 | tf_op jit(solution)/shard_map/all_gather | solution.py:113
  50.8 4.1 %copy.65 = bf16[256,4096]{1,0:T(8,128)(2,1)} copy(bf16[256,4096]{0,1:T(8,128)(2,1)} %bitcast.154) | data formatting | bytes 4194304 | tf_op jit(solution)/shard_map/dot_general | solution.py:69
  55.7 27.9 %all-gather.9.cloned.1.call-done = bf16[256,4096]{1,0:T(8,128)(2,1)} async-done(((bf16[256,1024]{1,0:T(8,128)(2,1)}), bf16[256,4096]{1,0:T(8,128)(2,1)}) %all-gather.9.cloned.1.call-update) | async-done | bytes 2097168 | tf_op jit(solution)/shard_map/all_gather | solution.py:64
  83.6 2.2 fusion.2
  86.5 1.3 copy-done.1
  88.7 14.3 %all_gather.36 = bf16[4,4,64,2,32]{2,4,0,3,1:T(8,128)(2,1)S(1)} all-gather(bf16[1,4,64,2,32]{2,4,0,3,1:T(8,128)(2,1)S(1)} %copy.44), channel_id=1, replica_groups=mesh['groups'=2,'mp'=4,'segment'=2,'section'=2] {'mp'}, dimensions={0}, use_global_device_ids=true | all-gather | bytes 163840 | tf_op jit(solution)/shard_map/all_gather | solution.py:73
  103.9 3.0 %fusion.89 = f32[4,64,2,128]{3,1,2,0:T(8,128)S(1)} fusion(bf16[4,64,4096,1]{2,1,3,0:T(8,128)(2,1)} %bitcast.149, bf16[2,128,4096,1]{2,1,0,3:T(8,128)(2,1)} %bitcast.151), kind=kOutput, calls=%fused_computation.133 | convolution fusion | flops 536870912 | bytes 4456448 | tf_op jit(solution)/shard_map/dot_general | solution.py:69
  109.3 1.9 fusion.83
  111.3 1.4 fusion.26
  112.8 14.7 %all_gather.37 = bf16[256,1024]{1,0:T(8,128)(2,1)S(1)} all-gather(bf16[256,256]{1,0:T(8,128)(2,1)S(1)} %bitcast.161), channel_id=1, replica_groups=mesh['groups'=2,'mp'=4,'segment'=2,'section'=2] {'mp'}, dimensions={1}, use_global_device_ids=true | all-gather | bytes 655360 | tf_op jit(solution)/shard_map/all_gather | solution.py:94
  128.2 3.4 %collective-permute-start = (bf16[256,1024]{1,0:T(8,128)(2,1)S(1)}, bf16[256,1024]{1,0:T(8,128)(2,1)S(1)}, u32[]{:S(2)}, u32[]{:S(2)}) collective-permute-start(bf16[256,1024]{1,0:T(8,128)(2,1)S(1)} %fusion.15), channel_id=1, source_target_pairs={{0,2},{1,3},{4,6},{5,7},{8,10},{9,11},{12,14},{13,15},{16,18},{17,... | collective-permute-start | bytes 1572872 | tf_op jit(solution)/shard_map/ppermute | solution.py:120
  131.6 6.6 %collective-permute-done = bf16[256,1024]{1,0:T(8,128)(2,1)S(1)} collective-permute-done((bf16[256,1024]{1,0:T(8,128)(2,1)S(1)}, bf16[256,1024]{1,0:T(8,128)(2,1)S(1)}, u32[]{:S(2)}, u32[]{:S(2)}) %collective-permute-start) | collective-permute-done | bytes 524320 | tf_op jit(solution)/shard_map/ppermute | solution.py:120
  139.1 46.4 %all-gather.11.cloned.1.call-done = bf16[256,4096]{1,0:T(8,128)(2,1)} async-done(((bf16[256,1024]{1,0:T(8,128)(2,1)}), bf16[256,4096]{1,0:T(8,128)(2,1)}) %all-gather.11.cloned.1.call-update) | async-done | bytes 2097168 | tf_op jit(solution)/shard_map/all_gather | solution.py:64
  185.5 2.2 fusion.5
  191.1 14.1 %all_gather.39 = bf16[4,4,64,2,32]{2,4,0,3,1:T(8,128)(2,1)S(1)} all-gather(bf16[1,4,64,2,32]{2,4,0,3,1:T(8,128)(2,1)S(1)} %copy.50), channel_id=1, replica_groups=mesh['groups'=2,'mp'=4,'segment'=2,'section'=2] {'mp'}, dimensions={0}, use_global_device_ids=true | all-gather | bytes 163840 | tf_op jit(solution)/shard_map/all_gather | solution.py:73
  206.9 1.2 fusion.86
  208.6 14.7 %all_gather.40 = bf16[256,1024]{1,0:T(8,128)(2,1)S(1)} all-gather(bf16[256,256]{1,0:T(8,128)(2,1)S(1)} %bitcast.162), channel_id=1, replica_groups=mesh['groups'=2,'mp'=4,'segment'=2,'section'=2] {'mp'}, dimensions={1}, use_global_device_ids=true | all-gather | bytes 655360 | tf_op jit(solution)/shard_map/all_gather | solution.py:94
  224.1 1.3 collective-permute-start.1
  225.5 6.9 %collective-permute-done.1 = bf16[4,32,1024]{2,1,0:T(8,128)(2,1)S(1)} collective-permute-done((bf16[4,32,1024]{2,1,0:T(8,128)(2,1)S(1)}, bf16[4,32,1024]{2,1,0:T(8,128)(2,1)S(1)}, u32[]{:S(2)}, u32[]{:S(2)}) %collective-permute-start.1) | collective-permute-done | bytes 262176 | tf_op jit(solution)/shard_map/ppermute | solution.py:127
  232.6 13.1 %all-gather.1 = f32[8,4,32]{2,1,0:T(4,128)S(1)} all-gather(f32[2,4,32]{2,1,0:T(4,128)S(1)} %pad_maximum_fusion), channel_id=3, replica_groups=mesh['groups'=2,'mp'=4,'segment'=2,'section'=2] {'mp'}, dimensions={0}, use_global_device_ids=true | all-gather | bytes 5120 | tf_op jit(solution)/shard_map/all_gather | solution.py:134
  245.7 4.3 %all-gather.2 = f32[2,32,4]{1,2,0:T(4,128)S(1)} all-gather(f32[1,32,4]{1,2,0:T(4,128)S(1)} %fusion.66), channel_id=1, replica_groups=mesh['groups'=2,'mp'=4,'segment'=2,'section'=2] {'segment'}, dimensions={0}, use_global_device_ids=true | all-gather | bytes 1536 | tf_op jit(solution)/shard_map/all_gather | solution.py:137
  (121 shorter events, 19.4 us)
Async XLA Ops:
  7.2 120.3 %copy-start = (bf16[1,1,1024,1024]{3,2,1,0:T(8,128)(2,1)S(1)}, bf16[1,1,1024,1024]{3,2,1,0:T(8,128)(2,1)}, u32[]{:S(2)}) copy-start(bf16[1,1,1024,1024]{3,2,1,0:T(8,128)(2,1)} %param.14) | copy-start | bytes 6291460
  7.2 26.4 %all-gather.7.cloned.1.call-start = ((), (), s32[]{:S(2)}) async-start(), calls=%async_computation | async-start | bytes 1572864 | tf_op jit(solution)/shard_map/all_gather | solution.py:110
  7.9 75.7 %all-gather.9.cloned.1.call-start = ((), (), s32[]{:S(2)}) async-start(), calls=%async_computation.1 | async-start | bytes 2621440 | tf_op jit(solution)/shard_map/all_gather | solution.py:64
  11.0 95.8 %copy-start.16 = (f32[4,64]{1,0:T(4,128)}, f32[4,64]{1,0:T(4,128)S(1)}, u32[]{:S(2)}) copy-start(f32[4,64]{1,0:T(4,128)S(1)} %get-tuple-element.20) | copy-start | bytes 3076
  33.6 3.9 %copy-start.20 = (bf16[1,1,1024]{2,1,0:T(2,128)(2,1)S(1)}, bf16[1,1,1024]{2,1,0:T(2,128)(2,1)}, u32[]{:S(2)}) copy-start(bf16[1,1,1024]{2,1,0:T(2,128)(2,1)} %param.15) | copy-start | bytes 6148
  37.5 148.1 %all-gather.11.cloned.1.call-start = ((), (), s32[]{:S(2)}) async-start(), calls=%async_computation.2 | async-start | bytes 2621440 | tf_op jit(solution)/shard_map/all_gather | solution.py:64
  55.0 51.9 %copy-start.24 = (f32[64]{0:T(128)}, f32[64]{0:T(128)S(1)}, u32[]{:S(2)}) copy-start(f32[64]{0:T(128)S(1)} %multiply_power_fusion) | copy-start | bytes 772
  83.6 2.2 copy-start.3
  85.9 2.0 copy-start.6
  103.9 4.4 %copy-start.11 = (pred[4,64,64]{1,2,0:T(8,128)(4,1)S(1)}, pred[4,64,64]{1,2,0:T(8,128)(4,1)}, u32[]{:S(2)}) copy-start(pred[4,64,64]{1,2,0:T(8,128)(4,1)} %compare_and_fusion) | copy-start | bytes 49156
  107.6 19.9 %copy-start.5 = (bf16[256,1024]{1,0:T(8,128)(2,1)S(1)}, bf16[256,1024]{1,0:T(8,128)(2,1)}, u32[]{:S(2)}) copy-start(bf16[256,1024]{1,0:T(8,128)(2,1)} %broadcast_select_fusion) | copy-start | bytes 1572868
  128.2 10.1 %collective-permute-start = (bf16[256,1024]{1,0:T(8,128)(2,1)S(1)}, bf16[256,1024]{1,0:T(8,128)(2,1)S(1)}, u32[]{:S(2)}, u32[]{:S(2)}) collective-permute-start(bf16[256,1024]{1,0:T(8,128)(2,1)S(1)} %fusion.15), channel_id=1, source_target_pairs={{0,2},{1,3},{4,6},{5,7},{8,10},{9,11},{12,14},{13,15},{16,18},{17,... | collective-permute-start | bytes 1572872 | tf_op jit(solution)/shard_map/ppermute | solution.py:120
  185.5 2.2 copy-start.4
  190.8 14.6 %copy-start.17 = (f32[4,64]{1,0:T(4,128)S(1)}, f32[4,64]{1,0:T(4,128)}, u32[]{:S(2)}) copy-start(f32[4,64]{1,0:T(4,128)} %copy-done.16) | copy-start | bytes 3076
  190.8 14.6 %copy-start.25 = (f32[64]{0:T(128)S(1)}, f32[64]{0:T(128)}, u32[]{:S(2)}) copy-start(f32[64]{0:T(128)} %copy-done.24) | copy-start | bytes 772
  190.8 15.8 %copy-start.12 = (pred[4,64,64]{1,2,0:T(8,128)(4,1)S(1)}, pred[4,64,64]{1,2,0:T(8,128)(4,1)}, u32[]{:S(2)}) copy-start(pred[4,64,64]{1,2,0:T(8,128)(4,1)} %compare_and_fusion) | copy-start | bytes 49156
  206.0 17.3 %copy-start.9 = (bf16[256,1024]{1,0:T(8,128)(2,1)S(1)}, bf16[256,1024]{1,0:T(8,128)(2,1)}, u32[]{:S(2)}) copy-start(bf16[256,1024]{1,0:T(8,128)(2,1)} %copy-done.8) | copy-start | bytes 1572868
  223.3 2.1 copy-start.21
  223.3 2.1 copy-start.22
  223.3 26.9 %copy-start.19 = (s32[4,4]{1,0:T(4,128)S(1)}, s32[4,4]{1,0:T(4,128)}, u32[]{:S(2)}) copy-start(s32[4,4]{1,0:T(4,128)} %get-tuple-element.18) | copy-start | bytes 196
  223.3 28.3 %copy-start.23 = (s32[16]{0:T(128)S(1)}, s32[16]{0:T(128)}, u32[]{:S(2)}) copy-start(s32[16]{0:T(128)} %param.11) | copy-start | bytes 196
  224.1 8.3 %collective-permute-start.1 = (bf16[4,32,1024]{2,1,0:T(8,128)(2,1)S(1)}, bf16[4,32,1024]{2,1,0:T(8,128)(2,1)S(1)}, u32[]{:S(2)}, u32[]{:S(2)}) collective-permute-start(bf16[4,32,1024]{2,1,0:T(8,128)(2,1)S(1)} %slice.78), channel_id=1, source_target_pairs={{2,0},{3,1},{6,4},{7,5},{10,8},{11,9},{14,12},{15,13},{18,16},{19,... | collective-permute-start | bytes 786440 | tf_op jit(solution)/shard_map/ppermute | solution.py:127
  250.2 2.1 copy-start.18
  250.3 1.2 collective-permute-start.2
  (8 other events, 6.9 us)
Sparse Core Ops, SparseCore 0:
  9.6 23.9 all-gather.6
  37.6 45.9 all-gather.8
  139.2 46.2 all-gather.10

commit v2 on v1

v2 whole, which is shorter than its diff:
```python
import functools

import jax
import jax.numpy as jnp
from jax import lax
from jax.experimental import pallas as pl
from jax.experimental.pallas import tpu as pltpu
from jax.sharding import PartitionSpec as P

D = 4096
HEAD_DIM = 128
GROUP = 8
MB = 4
R_MB = 4
T_MB = 64
LMAX = 32
RESP = 16


epsilon = 1e-06
rope_base = 1000000.0


def slot_tables(lengths, source):
    seg_ends = jnp.cumsum(lengths, axis=1)
    seg_starts = seg_ends - lengths
    places = jnp.arange(T_MB, dtype=jnp.int32)
    member = jnp.sum((places[None, :, None] >= seg_ends[:, None, :]).astype(jnp.int32), axis=2)
    one_hot = (member[:, :, None] == jnp.arange(R_MB, dtype=jnp.int32)[None, None, :]).astype(
        jnp.int32
    )
    position = places[None, :] - jnp.sum(one_hot * seg_starts[:, None, :], axis=2)
    owners = jnp.sum(one_hot * source.reshape(MB, R_MB)[:, None, :], axis=2)
    return (member, position, owners, seg_ends)


def angles(position):
    inv_freqs = rope_base ** (-jnp.arange(0, HEAD_DIM // 2, dtype=jnp.float32) * 2.0 / HEAD_DIM)
    phases = position.astype(jnp.float32)[..., None] * inv_freqs
    return (jnp.cos(phases), jnp.sin(phases))


def spin(block, cosine, signed_sine):
    return block * cosine + pltpu.roll(block, HEAD_DIM // 2, 1) * signed_sine


def stack_kernel(
    mp_count,
    seg_count,
    kv_width,
    resp,
    pick,
    code_col,
    base_col,
    code_row,
    cosine,
    signed_sine,
    gain,
    w_in,
    w_out,
    lift,
    lift_head,
    hidden,
    scores,
    other_scores,
    pool,
    x_own,
    x_all,
    gain_all,
    w_part,
    w_own,
    w_proj,
    part_out,
    part_in,
    acc,
    kv_all,
    att,
    y,
    y_in,
    stats,
    total,
    total_other,
    local_sem,
    pool_sem,
    gain_sem,
    half_sem,
    swap_sem,
    w_sem,
    part_sem,
    kv_sem,
    att_sem,
    next_sem,
    block_sem,
    stats_sem,
    total_sem,
    other_sem,
):
    f32, bf16 = jnp.float32, jnp.bfloat16
    me = lax.axis_index("mp")
    seg = lax.axis_index("segment")
    core = lax.axis_index("section")
    tokens, width = x_own.shape
    in_width = acc.shape[1]
    q_width = att.shape[1] // mp_count
    rows_pool = resp.shape[0]
    half = tokens // 2
    block = tokens // seg_count
    last = seg_count - 1
    group = HEAD_DIM // kv_width

    def peer(d):
        return lax.rem(me + d, mp_count)

    def source_of(d):
        return lax.rem(me + mp_count - d, mp_count)

    def remote(src, dst, sems, slot, **place):
        return pltpu.make_async_remote_copy(
            src_ref=src,
            dst_ref=dst,
            send_sem=sems.at[0, slot],
            recv_sem=sems.at[1, slot],
            device_id=place,
            device_id_type=pl.DeviceIdType.MESH,
        )

    barrier = pltpu.get_barrier_semaphore()
    for d in range(1, mp_count):
        pl.semaphore_signal(
            barrier, inc=1, device_id={"mp": peer(d)}, device_id_type=pl.DeviceIdType.MESH
        )
    for d in range(1, seg_count):
        pl.semaphore_signal(
            barrier,
            inc=1,
            device_id={"segment": lax.rem(seg + d, seg_count)},
            device_id_type=pl.DeviceIdType.MESH,
        )
    pl.semaphore_signal(
        barrier, inc=1, device_id={"section": 1 - core}, device_id_type=pl.DeviceIdType.MESH
    )
    proj_copy = pltpu.make_async_copy(w_out, w_proj, local_sem.at[0])
    proj_copy.start()
    pl.semaphore_wait(barrier, mp_count + seg_count - 1)

    def rows_of(index):
        return pl.ds(pl.multiple_of(index * width, width), width)

    lanes = lax.broadcasted_iota(jnp.int32, (tokens, in_width), 1)
    ss_lane = q_width + 2 * kv_width
    my_half = pl.ds(pl.multiple_of(core * half, half), half)
    its_half = pl.ds(pl.multiple_of((1 - core) * half, half), half)

    @pl.when(seg == 0)
    def _():
        own_w = pltpu.make_async_copy(w_in, w_own, local_sem.at[1])
        own_w.start()
        own_rows = pltpu.make_async_copy(resp, pool.at[0], local_sem.at[2])
        own_rows.start()
        gain_all[me] = gain[...]
        gain_copies = [
            remote(gain, gain_all.at[me], gain_sem, d, mp=peer(d)) for d in range(1, mp_count)
        ]
        for copy in gain_copies:
            copy.start()
        own_rows.wait()
        for s in range(1, seg_count):
            remote(resp, pool.at[s], pool_sem, s, segment=0).wait_recv()
        row_ids = lax.broadcasted_iota(jnp.int32, (tokens, rows_pool), 1)
        chosen = [
            (pick[...] - s * rows_pool == row_ids).astype(f32).astype(bf16) for s in range(seg_count)
        ]
        step = 256
        for at in range(0, width, step):
            found = jnp.dot(chosen[0], pool[0, :, at : at + step], preferred_element_type=f32)
            for s in range(1, seg_count):
                found += jnp.dot(chosen[s], pool[s, :, at : at + step], preferred_element_type=f32)
            x_own[:, at : at + step] = found.astype(bf16)
        halves = [
            remote(x_own.at[my_half], x_all.at[me, my_half], half_sem, d, mp=peer(d))
            for d in range(1, mp_count)
        ]
        for copy in halves:
            copy.start()
        own_w.wait()

        def shard(values, gains_row, index):
            rows = values.astype(f32)
            squares = jnp.sum(rows * rows, axis=1, keepdims=True)
            lifted = (rows * gains_row.astype(f32)).astype(bf16)
            product = jnp.dot(lifted, w_own[rows_of(index)], preferred_element_type=f32)
            return product + jnp.where(lanes == ss_lane, squares, 0.0)

        acc[...] = shard(x_own[...], gain[0:1], me)
        swaps = []
        for d in range(1, mp_count):
            halves[d - 1].wait_recv()
            here = x_all.at[source_of(d), my_half]
            swaps.append(remote(here, here, swap_sem, d, section=1 - core))
            swaps[-1].start()
        for d in range(1, mp_count):
            swaps[d - 1].wait_recv()
            gain_copies[d - 1].wait_recv()
            index = source_of(d)
            acc[...] += shard(x_all[index], gain_all[index, 0:1], index)
        for copy in halves + swaps + gain_copies:
            copy.wait_send()

    @pl.when(seg > 0)
    def _():
        rows_copy = remote(resp, pool.at[seg], pool_sem, seg, segment=0)
        rows_copy.start()
        own_w = pltpu.make_async_copy(w_in.at[rows_of(me)], w_part.at[me], local_sem.at[1])
        own_w.start()
        w_copies = [
            remote(w_in.at[rows_of(peer(d))], w_part.at[me], w_sem, d, mp=peer(d))
            for d in range(1, mp_count)
        ]
        for copy in w_copies:
            copy.start()
        own_w.wait()
        rows_copy.wait_send()
        for copy in w_copies:
            copy.wait()
        remote(y, x_own, next_sem, 0, segment=lax.rem(seg + 1, seg_count)).wait_recv()
        rows = x_own[...].astype(f32)
        squares = jnp.sum(rows * rows, axis=1, keepdims=True)
        upper = squares.astype(bf16).astype(f32)
        lower = squares - upper
        lifted = (rows * gain[0:1].astype(f32)).astype(bf16)
        extra = jnp.where(lanes == ss_lane, upper, jnp.where(lanes == ss_lane + 1, lower, 0.0))
        copies = []
        for d in range(1, mp_count):
            product = jnp.dot(lifted, w_part[peer(d)], preferred_element_type=f32)
            part_out[d] = (product + extra).astype(bf16)
            copies.append(remote(part_out.at[d], part_in.at[d], part_sem, d, mp=peer(d)))
            copies[-1].start()
        acc[...] = jnp.dot(lifted, w_part[me], preferred_element_type=f32) + extra
        for d in range(1, mp_count):
            copies[d - 1].wait_recv()
            acc[...] += part_in[d].astype(f32)
        for copy in copies:
            copy.wait_send()

    squares = acc[:, ss_lane : ss_lane + 1] + acc[:, ss_lane + 1 : ss_lane + 2]
    scale = lax.rsqrt(squares / D + epsilon)
    slot = lax.rem(me, group)
    kv_all[slot] = (acc[:, q_width:] * scale).astype(bf16)
    kv_copies = [
        remote(
            kv_all.at[slot], kv_all.at[slot], kv_sem, d, mp=me - slot + lax.rem(slot + d, group)
        )
        for d in range(1, group)
    ]
    for copy in kv_copies:
        copy.start()
    cos_here, sin_here = cosine[...], signed_sine[...]
    head_count = q_width // HEAD_DIM
    queries = []
    for h in range(head_count):
        vectors = acc[:, h * HEAD_DIM : (h + 1) * HEAD_DIM] * scale
        queries.append(spin(vectors, cos_here, sin_here).astype(bf16))
    codes = code_row[...]
    visible = (codes <= code_col[...]) & (codes >= base_col[...])
    for copy in kv_copies:
        copy.wait()
    kv_lanes = kv_all.shape[2]
    from_lane = lax.broadcasted_iota(jnp.int32, (kv_lanes, 2 * HEAD_DIM), 0)
    to_lane = lax.broadcasted_iota(jnp.int32, (kv_lanes, 2 * HEAD_DIM), 1)
    keyval = jnp.zeros((tokens, 2 * HEAD_DIM), f32)
    for g in range(group):
        place = jnp.where(
            from_lane < kv_width,
            from_lane + g * kv_width,
            from_lane - kv_width + HEAD_DIM + g * kv_width,
        )
        moved = (place == to_lane) & (from_lane < 2 * kv_width)
        keyval += jnp.dot(kv_all[g], moved.astype(f32).astype(bf16), preferred_element_type=f32)
    key_rows = spin(keyval[:, :HEAD_DIM], cos_here, sin_here).astype(bf16)
    value_rows = keyval[:, HEAD_DIM:].astype(bf16)
    outs = []
    for h in range(head_count):
        logits = lax.dot_general(
            queries[h], key_rows, (((1,), (1,)), ((), ())), preferred_element_type=f32
        ) * HEAD_DIM ** (-0.5)
        logits = jnp.where(visible, logits, -1e30)
        expo = jnp.exp(logits - jnp.max(logits, axis=1, keepdims=True))
        weights = (expo / jnp.sum(expo, axis=1, keepdims=True)).astype(bf16)
        outs.append(jnp.dot(weights, value_rows, preferred_element_type=f32).astype(bf16))
    my_columns = pl.ds(pl.multiple_of(me * q_width, q_width), q_width)
    att[:, my_columns] = jnp.concatenate(outs, axis=1)
    att_copies = [
        remote(att.at[:, my_columns], att.at[:, my_columns], att_sem, d, mp=peer(d))
        for d in range(1, mp_count)
    ]
    for copy in att_copies:
        copy.start()
    proj_copy.wait()
    for copy in att_copies:
        copy.wait()
    step = 256
    for at in range(0, width, step):
        projected = jnp.dot(att[...], w_proj[:, at : at + step], preferred_element_type=f32)
        y[:, at : at + step] = (x_own[:, at : at + step].astype(f32) + projected).astype(bf16)

    @pl.when(seg < last)
    def _():
        onward = remote(y, x_own, next_sem, 0, segment=lax.rem(seg + 1, seg_count))
        onward.start()
        onward.wait_send()
        remote(y.at[pl.ds(0, block)], y_in, block_sem, seg, segment=0).wait_recv()
        remote(total, total, total_sem, seg, segment=0).wait_recv()

    @pl.when(seg == last)
    def _():
        blocks = [
            remote(y.at[pl.ds(i * block, block)], y_in, block_sem, i, segment=i)
            for i in range(last)
        ]
        for copy in blocks:
            copy.start()
        rows = y[...].astype(f32)
        squares = jnp.sum(rows * rows, axis=1, keepdims=True)
        dots = jnp.sum(rows * lift_head[...], axis=1, keepdims=True)
        lane = lax.broadcasted_iota(jnp.int32, (tokens, HEAD_DIM), 1)
        both = jnp.where(lane == 0, squares, jnp.where(lane == 1, dots, 0.0))
        stats[0] = jnp.transpose(both)[:8]
        copies = [
            remote(stats.at[0], stats.at[d], stats_sem, d, mp=peer(d)) for d in range(1, mp_count)
        ]
        for copy in copies:
            copy.start()
        for copy in copies:
            copy.wait()
        total[...] = jnp.sum(stats[...], axis=0)
        totals = [remote(total, total, total_sem, i, segment=i) for i in range(last)]
        for copy in totals:
            copy.start()
        for copy in blocks + totals:
            copy.wait_send()
        y_in[...] = y[last * block : (last + 1) * block]

    swap = remote(total, total_other, other_sem, 0, section=1 - core)
    swap.start()
    row_scale = lax.rsqrt(total[0:1] / D + epsilon)
    scores[...] = jnp.broadcast_to(total[1:2] * row_scale, scores.shape)
    at_token = lax.broadcasted_iota(jnp.int32, (block, tokens), 1)
    wanted = lax.broadcasted_iota(jnp.int32, (block, tokens), 0) + seg * block
    column = jnp.sum(jnp.where(at_token == wanted, row_scale, 0.0), axis=1, keepdims=True)
    hidden[...] = (y_in[...].astype(f32) * column * lift[...]).astype(bf16)
    swap.wait()
    other_scores[...] = jnp.broadcast_to(
        total_other[1:2] * lax.rsqrt(total_other[0:1] / D + epsilon), other_scores.shape
    )


def per_device(resp_rows, lengths, source, w_query, w_keyval, w_out, gains, final_gain, head):
    seg_count = lax.axis_size("segment")
    mp_count = lax.axis_size("mp")
    f32, bf16 = jnp.float32, jnp.bfloat16
    member, position, owners, seg_ends = slot_tables(lengths, source)
    width = resp_rows.shape[2]
    rows_here = T_MB // seg_count
    tokens = MB * T_MB
    block = tokens // seg_count

    def ordered(table):
        return table.reshape(MB, seg_count, rows_here).transpose(1, 0, 2).reshape(-1)

    slots = ordered(member + R_MB * jnp.arange(MB, dtype=jnp.int32)[:, None])
    spots = ordered(position)
    pick = ordered(owners) * LMAX + spots
    base = slots * T_MB
    code = base + spots
    cosine, sine_part = angles(spots)
    cosine = jnp.concatenate([cosine, cosine], axis=1)
    signed_sine = jnp.concatenate([-sine_part, sine_part], axis=1)
    kv_width = w_keyval.shape[-1]
    q_width = w_query.shape[-1]
    kv_lanes = HEAD_DIM
    keyval_w = w_keyval[0, 0].reshape(D, 2 * kv_width)
    w_in = jnp.concatenate(
        [w_query[0, 0], keyval_w, jnp.zeros((D, kv_lanes - 2 * kv_width), bf16)], axis=1
    )
    in_width = q_width + kv_lanes
    lift = final_gain.astype(f32)
    rows_pool = resp_rows.shape[0] * LMAX
    vmem = pl.BlockSpec(memory_space=pltpu.VMEM)
    hbm = pl.BlockSpec(memory_space=pl.ANY)
    group = HEAD_DIM // kv_width
    dma = pltpu.SemaphoreType.DMA
    hidden, scores, other = pl.pallas_call(
        functools.partial(stack_kernel, mp_count, seg_count, kv_width),
        out_shape=(
            jax.ShapeDtypeStruct((block, width), bf16),
            jax.ShapeDtypeStruct((8, tokens), f32),
            jax.ShapeDtypeStruct((8, tokens), f32),
        ),
        in_specs=[hbm, vmem, vmem, vmem, vmem, vmem, vmem, vmem, hbm, hbm, vmem, vmem],
        out_specs=(vmem, vmem, vmem),
        scratch_shapes=[
            pltpu.VMEM((seg_count, rows_pool, width), bf16),
            pltpu.VMEM((tokens, width), bf16),
            pltpu.VMEM((mp_count, tokens, width), bf16),
            pltpu.VMEM((mp_count, 16, width), bf16),
            pltpu.VMEM((mp_count, width, in_width), bf16),
            pltpu.VMEM((D, in_width), bf16),
            pltpu.VMEM((mp_count * q_width, width), bf16),
            pltpu.VMEM((mp_count, tokens, in_width), bf16),
            pltpu.VMEM((mp_count, tokens, in_width), bf16),
            pltpu.VMEM((tokens, in_width), f32),
            pltpu.VMEM((group, tokens, kv_lanes), bf16),
            pltpu.VMEM((tokens, mp_count * q_width), bf16),
            pltpu.VMEM((tokens, width), bf16),
            pltpu.VMEM((block, width), bf16),
            pltpu.VMEM((mp_count, 8, tokens), f32),
            pltpu.VMEM((8, tokens), f32),
            pltpu.VMEM((8, tokens), f32),
            dma((3,)),
            dma((2, seg_count)),
            dma((2, mp_count)),
            dma((2, mp_count)),
            dma((2, mp_count)),
            dma((2, mp_count)),
            dma((2, mp_count)),
            dma((2, group)),
            dma((2, mp_count)),
            dma((2, 1)),
            dma((2, seg_count)),
            dma((2, mp_count)),
            dma((2, seg_count)),
            dma((2, 1)),
        ],
        compiler_params=pltpu.CompilerParams(
            collective_id=0, has_side_effects=True, vmem_limit_bytes=44 * 1024 * 1024
        ),
    )(
        resp_rows.reshape(rows_pool, width),
        pick[:, None],
        code[:, None],
        base[:, None],
        code[None, :],
        cosine,
        signed_sine,
        jnp.broadcast_to(gains[0], (16, width)),
        w_in,
        w_out[0, 0],
        lift,
        lift * head.astype(f32),
    )

    def restored(row):
        return row.reshape(seg_count, MB, rows_here).transpose(1, 0, 2).reshape(MB, T_MB)

    scores, other = restored(scores[0]), restored(other[0])
    hidden = hidden.reshape(1, MB, rows_here, width)
    places = jnp.arange(T_MB, dtype=jnp.int32)
    last_pick = (places[None, None, :] == (seg_ends - 1)[:, :, None]).astype(f32)
    section_no = lax.axis_index("section")
    gap = jnp.where(section_no == 0, scores - other, other - scores)
    gap_slot = jnp.sum(last_pick * gap[:, None, :], axis=-1).reshape(-1)
    half_count = RESP // 2
    response_ids = section_no * half_count + jnp.arange(half_count, dtype=jnp.int32)
    matches = (source[None, :] == response_ids[:, None]).astype(f32)
    own_part = jnp.sum(matches * gap_slot[None, :], axis=1)
    return (hidden, scores[None], own_part)


def solution(mesh):
    in_specs = (
        P(("groups", "segment"), None, "mp"),
        P("groups", None),
        P("groups"),
        P("section", "segment", None, "mp"),
        P("section", "segment", None, None, "mp"),
        P("section", "segment", None, "mp"),
        P("section", "segment", "mp"),
        P("section", "mp"),
        P("section", "mp"),
    )
    out_specs = (
        P("section", "groups", "segment", "mp"),
        P("section", "groups", None),
        P(("groups", "section")),
    )
    return jax.shard_map(
        per_device, mesh=mesh, in_specs=in_specs, out_specs=out_specs, check_vma=False
    )
```

time: 259 us -> 150 us (0.58)
  Pallas kernels: 0 us -> 127 us
  waiting for transfers between devices: 111 us -> 0 us
  blocking collectives: 88.6 us -> 0 us
  between operations: 14.3 us -> 0.72 us
  matrix products: 12.8 us -> 0 us
  other arithmetic: 13.2 us -> 8.04 us
  starting transfers between devices: 4.81 us -> 0 us
    pallas_call x0 -> x1, Pallas kernels: none -> 127 us  [per_device(): pl.pallas_call(functools.partial(stack_kernel, mp_count, seg_count, kv_wi...]
    all_gather x3 -> x0, waiting for transfers between devices: 96.7 us -> none  [the longest x2 74.4 us: layer(): whole = lax.all_gather(tok_rows, 'mp', axis=1, tiled=True)]
    all_gather x7 -> x0, blocking collectives: 88.6 us -> none  [the longest x2 29.4 us: layer(): lax.all_gather(attended, 'mp', axis=1, tiled=True)]
    ppermute x3 -> x0, waiting for transfers between devices: 13.8 us -> none  [the longest x1 6.88 us: per_device(): came = lax.ppermute(blocks[i], 'segment', [(last, i)])]
    dot_general x10 -> x0, matrix products: 9.64 us -> none  [the longest x2 3.7 us: layer(): queries = jnp.dot(normed, query_w, preferred_element_type=jnp.float32)]
    ppermute x3 -> x0, starting transfers between devices: 4.69 us -> none  [the longest x1 3.4 us: per_device(): x = lax.ppermute(y, 'segment', [(step, step + 1)])]
    reduce_sum x5 -> x1, other arithmetic: 4.85 us -> 0.16 us  [per_device(): gap_slot = jnp.sum(last_pick * gap[:, None, :], axis=-1).reshape(-1)]
    dot_general x1 -> x0, local copies, waits for them, and re-layouts: 4.13 us -> none  [layer(): queries = jnp.dot(normed, query_w, preferred_element_type=jnp.float32)]
  transfers between devices with their start and end apart: 6 -> 0, of which waited for: 6 -> 0; matrix products, arithmetic and copies ran while one was open for 3% -> 0% of each run, Pallas kernels for 0% -> 0%
where the time goes in v2:
time: 150 us; the launch traced here: 149 us
  Pallas kernels  127 us (85%)
  local copies, waits for them, and re-layouts  13.5 us (9%)
  other arithmetic  8.04 us (5%)
    pallas_call x1, Pallas kernels, per_device(): pl.pallas_call(functools.partial(stack_kernel, mp_count, seg_count, kv_wi...  127 us
    unnamed x13, local copies, waits for them, and re-layouts  6.79 us

profile of v2, /device:TPU:0, one launch (start us, length us, event | category | flops | bytes accessed | tf_op | source)
XLA Modules:
  0.0 149.1 jit_solution(13701671320771513780)
XLA Ops:
  0.6 0.9 reduce_window_sum.11
  1.5 0.7 broadcast_add_fusion
  2.2 0.1 convert_reduce_fusion
  2.3 0.7 mul.120
  3.0 0.1 select_reduce_fusion.1
  3.3 0.5 fusion
  3.8 0.1 pad_maximum_fusion
  4.5 0.1 copy.56.pick
  4.6 0.8 copy.57.code_col
  5.4 0.8 copy.58.base_col
  6.3 2.4 %copy.55 = bf16[4096,64]{1,0:T(8,128)(2,1)} copy(bf16[4096,64]{0,1:T(8,128)(2,1)} %bitcast.28) | data formatting | bytes 1048576 | tf_op jit(solution)/shard_map/reshape;squeeze | solution.py:381
  8.8 2.6 %maximum_maximum_fusion.w_in = bf16[4096,384]{1,0:T(8,128)(2,1)S(1)} fusion(bf16[4096,64]{1,0:T(8,128)(2,1)} %copy.55, bf16[4096,256]{1,0:T(8,128)(2,1)} %bitcast.27, bf16[384]{0:T(512)(128)(2,1)S(1)} %pad.2.clone), kind=kLoop, calls=%fused_computation | loop fusion | flops 9437184 | bytes 5767936 | tf_op jit(solution)/shard_map/concatenate | solution.py:382
  11.4 0.7 reduce
  12.1 0.7 convert_multiply_fusion.lift_head
  12.8 1.6 %copy-done = bf16[1,1,1024,1024]{3,2,1,0:T(8,128)(2,1)S(1)} copy-done((bf16[1,1,1024,1024]{3,2,1,0:T(8,128)(2,1)S(1)}, bf16[1,1,1024,1024]{3,2,1,0:T(8,128)(2,1)}, u32[]{:S(2)}) %copy-start) | copy-done | bytes 2097176
  14.4 0.9 copy-done.1
  15.3 0.9 copy-done.2
  16.2 1.0 copy-done.3
  17.3 126.9 %shard_map.112 = (bf16[128,1024]{1,0:T(8,128)(2,1)S(1)}, f32[8,256]{1,0:T(8,128)S(1)}, f32[8,256]{1,0:T(8,128)S(1)}) custom-call(bf16[256,1024]{1,0:T(8,128)(2,1)S(1)} %bitcast.25, s32[256,1]{1,0:T(8,128)S(1)} %copy.56.pick, s32[256,1]{1,0:T(8,128)S(1)} %copy-done.1, s32[256,1]{1,0:T(8,128)S(1)} %copy-done.2, s32[1,256]{1,0:T(1,128)S(1)} %add.65.code_row, ...), custom_call_target="tpu_custom_call" | custom-call | tf_op jit(solution)/shard_map/pallas_call | solution.py:392
  144.2 0.7 copy-done.4
  145.1 0.2 select_reduce_fusion
  145.4 1.4 select_reduce_fusion.3
  146.8 0.7 broadcast_in_dim_reshape.2
  147.4 1.7 %copy.77 = bf16[1,4,32,1024]{3,2,1,0:T(8,128)(2,1)} copy(bf16[1,4,32,1024]{3,2,1,0:T(8,128)(2,1)} %bitcast.26) | data formatting | bytes 524288
  (36 shorter events, 1.3 us)
Async XLA Ops:
  8.8 3.3 %copy-start.5 = (bf16[1,1024]{1,0:T(2,128)(2,1)S(1)}, bf16[1,1024]{1,0:T(2,128)(2,1)}, u32[]{:S(2)}) copy-start(bf16[1,1024]{1,0:T(2,128)(2,1)} %param.16) | copy-start | bytes 6148
  12.8 1.6 %copy-start = (bf16[1,1,1024,1024]{3,2,1,0:T(8,128)(2,1)S(1)}, bf16[1,1,1024,1024]{3,2,1,0:T(8,128)(2,1)}, u32[]{:S(2)}) copy-start(bf16[1,1,1024,1024]{3,2,1,0:T(8,128)(2,1)} %param.14) | copy-start | bytes 6291460
  14.4 0.9 copy-start.1
  15.3 0.9 copy-start.2
  16.2 1.0 copy-start.3
  144.2 0.7 copy-start.4

commit v3 on v2

--- a/solution.py
+++ b/solution.py
@@ -51,15 +51,15 @@
     resp,
     pick,
     code_col,
-    base_col,
     code_row,
     cosine,
     signed_sine,
     gain,
-    w_in,
+    w_query,
+    w_keyval,
     w_out,
-    lift,
-    lift_head,
+    final_gain,
+    head,
     hidden,
     scores,
     other_scores,
@@ -67,8 +67,10 @@
     x_own,
     x_all,
     gain_all,
-    w_part,
-    w_own,
+    query_part,
+    keyval_part,
+    query_own,
+    keyval_own,
     w_proj,
     part_out,
     part_in,
@@ -86,6 +88,7 @@
     half_sem,
     swap_sem,
     w_sem,
+    share_sem,
     part_sem,
     kv_sem,
     att_sem,
@@ -99,11 +102,13 @@
     me = lax.axis_index("mp")
     seg = lax.axis_index("segment")
     core = lax.axis_index("section")
+    team = lax.axis_index("groups")
     tokens, width = x_own.shape
     in_width = acc.shape[1]
     q_width = att.shape[1] // mp_count
     rows_pool = resp.shape[0]
     half = tokens // 2
+    half_width = width // 2
     block = tokens // seg_count
     last = seg_count - 1
     group = HEAD_DIM // kv_width
@@ -139,106 +144,171 @@
     pl.semaphore_signal(
         barrier, inc=1, device_id={"section": 1 - core}, device_id_type=pl.DeviceIdType.MESH
     )
+    pl.semaphore_signal(
+        barrier, inc=1, device_id={"groups": 1 - team}, device_id_type=pl.DeviceIdType.MESH
+    )
     proj_copy = pltpu.make_async_copy(w_out, w_proj, local_sem.at[0])
     proj_copy.start()
-    pl.semaphore_wait(barrier, mp_count + seg_count - 1)
+    pl.semaphore_wait(barrier, mp_count + seg_count)
 
     def rows_of(index):
         return pl.ds(pl.multiple_of(index * width, width), width)
 
-    lanes = lax.broadcasted_iota(jnp.int32, (tokens, in_width), 1)
     ss_lane = q_width + 2 * kv_width
-    my_half = pl.ds(pl.multiple_of(core * half, half), half)
-    its_half = pl.ds(pl.multiple_of((1 - core) * half, half), half)
+    kv_lanes = in_width - q_width
+    my_columns = pl.ds(pl.multiple_of(core * half_width, half_width), half_width)
 
     @pl.when(seg == 0)
     def _():
-        own_w = pltpu.make_async_copy(w_in, w_own, local_sem.at[1])
-        own_w.start()
-        own_rows = pltpu.make_async_copy(resp, pool.at[0], local_sem.at[2])
+        own_rows = pltpu.make_async_copy(resp.at[:, my_columns], pool.at[0], local_sem.at[3])
         own_rows.start()
+        own_query = pltpu.make_async_copy(w_query, query_own, local_sem.at[1])
+        own_query.start()
+        own_keyval = pltpu.make_async_copy(w_keyval, keyval_own, local_sem.at[2])
+        own_keyval.start()
         gain_all[me] = gain[...]
         gain_copies = [
             remote(gain, gain_all.at[me], gain_sem, d, mp=peer(d)) for d in range(1, mp_count)
         ]
         for copy in gain_copies:
             copy.start()
-        own_rows.wait()
-        for s in range(1, seg_count):
-            remote(resp, pool.at[s], pool_sem, s, segment=0).wait_recv()
         row_ids = lax.broadcasted_iota(jnp.int32, (tokens, rows_pool), 1)
         chosen = [
             (pick[...] - s * rows_pool == row_ids).astype(f32).astype(bf16) for s in range(seg_count)
         ]
-        step = 256
-        for at in range(0, width, step):
+        own_rows.wait()
+        for s in range(1, seg_count):
+            remote(resp.at[:, my_columns], pool.at[s], pool_sem, s, segment=0).wait_recv()
+        step = min(256, half_width)
+        for at in range(0, half_width, step):
             found = jnp.dot(chosen[0], pool[0, :, at : at + step], preferred_element_type=f32)
             for s in range(1, seg_count):
                 found += jnp.dot(chosen[s], pool[s, :, at : at + step], preferred_element_type=f32)
-            x_own[:, at : at + step] = found.astype(bf16)
+            x_own[:, pl.ds(pl.multiple_of(core * half_width + at, step), step)] = found.astype(bf16)
+        packed = x_own.at[:, my_columns]
         halves = [
-            remote(x_own.at[my_half], x_all.at[me, my_half], half_sem, d, mp=peer(d))
+            remote(packed, x_all.at[me, :, my_columns], half_sem, d, mp=peer(d))
             for d in range(1, mp_count)
         ]
         for copy in halves:
             copy.start()
-        own_w.wait()
+        swaps = [remote(packed, packed, swap_sem, 0, section=1 - core)]
+        swaps[0].start()
+        own_query.wait()
+        own_keyval.wait()
+        lane = lax.broadcasted_iota(jnp.int32, (tokens, kv_lanes), 1)
 
         def shard(values, gains_row, index):
             rows = values.astype(f32)
             squares = jnp.sum(rows * rows, axis=1, keepdims=True)
             lifted = (rows * gains_row.astype(f32)).astype(bf16)
-            product = jnp.dot(lifted, w_own[rows_of(index)], preferred_element_type=f32)
-            return product + jnp.where(lanes == ss_lane, squares, 0.0)
-
-        acc[...] = shard(x_own[...], gain[0:1], me)
-        swaps = []
+            at = rows_of(index)
+            acc[:, :q_width] += jnp.dot(lifted, query_own[at], preferred_element_type=f32)
+            keyval = jnp.dot(lifted, keyval_own[at], preferred_element_type=f32)
+            acc[:, q_width:] += keyval + jnp.where(lane == 2 * kv_width, squares, 0.0)
+
+        def add(d):
+            swaps[d].wait_recv()
+            if d == 0:
+                shard(x_own[...], gain[0:1], me)
+            else:
+                gain_copies[d - 1].wait_recv()
+                index = source_of(d)
+                shard(x_all[index], gain_all[index, 0:1], index)
+
+        acc[...] = jnp.zeros_like(acc)
         for d in range(1, mp_count):
+            here = x_all.at[source_of(d), :, my_columns]
+            swaps.append(remote(here, here, swap_sem, d, section=1 - core))
+        order = []
+        for d in range(1, mp_count // 2 + 1):
+            order += [d] if 2 * d == mp_count else [d, mp_count - d]
+        done = 0
+        for d in order:
             halves[d - 1].wait_recv()
-            here = x_all.at[source_of(d), my_half]
-            swaps.append(remote(here, here, swap_sem, d, section=1 - core))
-            swaps[-1].start()
-        for d in range(1, mp_count):
-            swaps[d - 1].wait_recv()
-            gain_copies[d - 1].wait_recv()
-            index = source_of(d)
-            acc[...] += shard(x_all[index], gain_all[index, 0:1], index)
+            swaps[d].start()
+            add(done)
+            done = d
+        add(done)
         for copy in halves + swaps + gain_copies:
             copy.wait_send()
 
     @pl.when(seg > 0)
     def _():
-        rows_copy = remote(resp, pool.at[seg], pool_sem, seg, segment=0)
+        rows_copy = remote(resp.at[:, my_columns], pool.at[seg], pool_sem, seg, segment=0)
         rows_copy.start()
-        own_w = pltpu.make_async_copy(w_in.at[rows_of(me)], w_part.at[me], local_sem.at[1])
-        own_w.start()
-        w_copies = [
-            remote(w_in.at[rows_of(peer(d))], w_part.at[me], w_sem, d, mp=peer(d))
-            for d in range(1, mp_count)
-        ]
-        for copy in w_copies:
+        upper_rows = pl.ds(pl.multiple_of(team * half_width, half_width), half_width)
+        weights = [(w_query, query_part), (w_keyval, keyval_part)]
+        shards = []
+        shares = []
+        for i, (whole, part) in enumerate(weights):
+            for d in range(1, mp_count):
+                rows = pl.ds(
+                    pl.multiple_of(peer(d) * width + team * half_width, half_width), half_width
+                )
+                here = part.at[source_of(d), upper_rows]
+                slot = i * mp_count + d
+                shards.append(
+                    remote(whole.at[rows], part.at[me, upper_rows], w_sem, slot, mp=peer(d))
+                )
+                shares.append(remote(here, here, share_sem, slot, groups=1 - team))
+        for copy in shards:
             copy.start()
-        own_w.wait()
+        for i, (whole, part) in enumerate(weights):
+            own = pltpu.make_async_copy(whole.at[rows_of(me)], part.at[me], local_sem.at[1 + i])
+            own.start()
+            own.wait()
         rows_copy.wait_send()
-        for copy in w_copies:
-            copy.wait()
-        remote(y, x_own, next_sem, 0, segment=lax.rem(seg + 1, seg_count)).wait_recv()
-        rows = x_own[...].astype(f32)
-        squares = jnp.sum(rows * rows, axis=1, keepdims=True)
-        upper = squares.astype(bf16).astype(f32)
-        lower = squares - upper
-        lifted = (rows * gain[0:1].astype(f32)).astype(bf16)
-        extra = jnp.where(lanes == ss_lane, upper, jnp.where(lanes == ss_lane + 1, lower, 0.0))
+        for copy, share in zip(shards, shares):
+            copy.wait_recv()
+            share.start()
+        for share in shares:
+            share.wait()
+        for copy in shards:
+            copy.wait_send()
+        lane = lax.broadcasted_iota(jnp.int32, (half, kv_lanes), 1)
         copies = []
-        for d in range(1, mp_count):
-            product = jnp.dot(lifted, w_part[peer(d)], preferred_element_type=f32)
-            part_out[d] = (product + extra).astype(bf16)
-            copies.append(remote(part_out.at[d], part_in.at[d], part_sem, d, mp=peer(d)))
-            copies[-1].start()
-        acc[...] = jnp.dot(lifted, w_part[me], preferred_element_type=f32) + extra
-        for d in range(1, mp_count):
-            copies[d - 1].wait_recv()
-            acc[...] += part_in[d].astype(f32)
+        for r in range(2):
+            mine = pl.ds(r * half, half)
+            remote(
+                y.at[mine], x_own.at[mine], next_sem, r, segment=lax.rem(seg + 1, seg_count)
+            ).wait_recv()
+            rows = x_own[mine].astype(f32)
+            squares = jnp.sum(rows * rows, axis=1, keepdims=True)
+            upper = squares.astype(bf16).astype(f32)
+            extra = jnp.where(
+                lane == 2 * kv_width,
+                upper,
+                jnp.where(lane == 2 * kv_width + 1, squares - upper, 0.0),
+            )
+            lifted = (rows * gain[0:1].astype(f32)).astype(bf16)
+            for d in range(1, mp_count):
+                index = peer(d)
+                part_out[d, mine, :q_width] = jnp.dot(
+                    lifted, query_part[index], preferred_element_type=f32
+                ).astype(bf16)
+                part_out[d, mine, q_width:] = (
+                    jnp.dot(lifted, keyval_part[index], preferred_element_type=f32) + extra
+                ).astype(bf16)
+                copies.append(
+                    remote(
+                        part_out.at[d, mine],
+                        part_in.at[d, mine],
+                        part_sem,
+                        r * mp_count + d,
+                        mp=index,
+                    )
+                )
+                copies[-1].start()
+            acc[mine, :q_width] = jnp.dot(lifted, query_part[me], preferred_element_type=f32)
+            acc[mine, q_width:] = (
+                jnp.dot(lifted, keyval_part[me], preferred_element_type=f32) + extra
+            )
+        for r in range(2):
+            mine = pl.ds(r * half, half)
+            for d in range(1, mp_count):
+                copies[r * (mp_count - 1) + d - 1].wait_recv()
+                acc[mine] += part_in[d, mine].astype(f32)
         for copy in copies:
             copy.wait_send()
 
@@ -261,10 +331,9 @@
         vectors = acc[:, h * HEAD_DIM : (h + 1) * HEAD_DIM] * scale
         queries.append(spin(vectors, cos_here, sin_here).astype(bf16))
     codes = code_row[...]
-    visible = (codes <= code_col[...]) & (codes >= base_col[...])
+    visible = (codes <= code_col[...]) & (codes >= code_col[...] // T_MB * T_MB)
     for copy in kv_copies:
         copy.wait()
-    kv_lanes = kv_all.shape[2]
     from_lane = lax.broadcasted_iota(jnp.int32, (kv_lanes, 2 * HEAD_DIM), 0)
     to_lane = lax.broadcasted_iota(jnp.int32, (kv_lanes, 2 * HEAD_DIM), 1)
     keyval = jnp.zeros((tokens, 2 * HEAD_DIM), f32)
@@ -287,10 +356,10 @@
         expo = jnp.exp(logits - jnp.max(logits, axis=1, keepdims=True))
         weights = (expo / jnp.sum(expo, axis=1, keepdims=True)).astype(bf16)
         outs.append(jnp.dot(weights, value_rows, preferred_element_type=f32).astype(bf16))
-    my_columns = pl.ds(pl.multiple_of(me * q_width, q_width), q_width)
-    att[:, my_columns] = jnp.concatenate(outs, axis=1)
+    att_columns = pl.ds(pl.multiple_of(me * q_width, q_width), q_width)
+    att[:, att_columns] = jnp.concatenate(outs, axis=1)
     att_copies = [
-        remote(att.at[:, my_columns], att.at[:, my_columns], att_sem, d, mp=peer(d))
+        remote(att.at[:, att_columns], att.at[:, att_columns], att_sem, d, mp=peer(d))
         for d in range(1, mp_count)
     ]
     for copy in att_copies:
@@ -299,15 +368,34 @@
     for copy in att_copies:
         copy.wait()
     step = 256
-    for at in range(0, width, step):
-        projected = jnp.dot(att[...], w_proj[:, at : at + step], preferred_element_type=f32)
-        y[:, at : at + step] = (x_own[:, at : at + step].astype(f32) + projected).astype(bf16)
+
+    def onward(r):
+        mine = pl.ds(r * half, half)
+        return remote(
+            y.at[mine], x_own.at[mine], next_sem, r, segment=lax.rem(seg + 1, seg_count)
+        )
+
+    for r in range(2):
+        mine = pl.ds(r * half, half)
+        for at in range(0, width, step):
+            projected = jnp.dot(
+                att[mine], w_proj[:, at : at + step], preferred_element_type=f32
+            )
+            y[mine, at : at + step] = (
+                x_own[mine, at : at + step].astype(f32) + projected
+            ).astype(bf16)
+
+        @pl.when(seg < last)
+        def _():
+            onward(r).start()
+
+    lift = final_gain[...].astype(f32)
+    lift_head = lift * head[...].astype(f32)
 
     @pl.when(seg < last)
     def _():
-        onward = remote(y, x_own, next_sem, 0, segment=lax.rem(seg + 1, seg_count))
-        onward.start()
-        onward.wait_send()
+        for r in range(2):
+            onward(r).wait_send()
         remote(y.at[pl.ds(0, block)], y_in, block_sem, seg, segment=0).wait_recv()
         remote(total, total, total_sem, seg, segment=0).wait_recv()
 
@@ -321,7 +409,7 @@
             copy.start()
         rows = y[...].astype(f32)
         squares = jnp.sum(rows * rows, axis=1, keepdims=True)
-        dots = jnp.sum(rows * lift_head[...], axis=1, keepdims=True)
+        dots = jnp.sum(rows * lift_head, axis=1, keepdims=True)
         lane = lax.broadcasted_iota(jnp.int32, (tokens, HEAD_DIM), 1)
         both = jnp.where(lane == 0, squares, jnp.where(lane == 1, dots, 0.0))
         stats[0] = jnp.transpose(both)[:8]
@@ -347,7 +435,7 @@
     at_token = lax.broadcasted_iota(jnp.int32, (block, tokens), 1)
     wanted = lax.broadcasted_iota(jnp.int32, (block, tokens), 0) + seg * block
     column = jnp.sum(jnp.where(at_token == wanted, row_scale, 0.0), axis=1, keepdims=True)
-    hidden[...] = (y_in[...].astype(f32) * column * lift[...]).astype(bf16)
+    hidden[...] = (y_in[...].astype(f32) * column * lift).astype(bf16)
     swap.wait()
     other_scores[...] = jnp.broadcast_to(
         total_other[1:2] * lax.rsqrt(total_other[0:1] / D + epsilon), other_scores.shape
@@ -370,8 +458,7 @@
     slots = ordered(member + R_MB * jnp.arange(MB, dtype=jnp.int32)[:, None])
     spots = ordered(position)
     pick = ordered(owners) * LMAX + spots
-    base = slots * T_MB
-    code = base + spots
+    code = slots * T_MB + spots
     cosine, sine_part = angles(spots)
     cosine = jnp.concatenate([cosine, cosine], axis=1)
     signed_sine = jnp.concatenate([-sine_part, sine_part], axis=1)
@@ -379,11 +466,8 @@
     q_width = w_query.shape[-1]
     kv_lanes = HEAD_DIM
     keyval_w = w_keyval[0, 0].reshape(D, 2 * kv_width)
-    w_in = jnp.concatenate(
-        [w_query[0, 0], keyval_w, jnp.zeros((D, kv_lanes - 2 * kv_width), bf16)], axis=1
-    )
+    keyval_w = jnp.pad(keyval_w, ((0, 0), (0, kv_lanes - 2 * kv_width)))
     in_width = q_width + kv_lanes
-    lift = final_gain.astype(f32)
     rows_pool = resp_rows.shape[0] * LMAX
     vmem = pl.BlockSpec(memory_space=pltpu.VMEM)
     hbm = pl.BlockSpec(memory_space=pl.ANY)
@@ -396,15 +480,17 @@
             jax.ShapeDtypeStruct((8, tokens), f32),
             jax.ShapeDtypeStruct((8, tokens), f32),
         ),
-        in_specs=[hbm, vmem, vmem, vmem, vmem, vmem, vmem, vmem, hbm, hbm, vmem, vmem],
+        in_specs=[hbm] + [vmem] * 6 + [hbm] * 3 + [vmem] * 2,
         out_specs=(vmem, vmem, vmem),
         scratch_shapes=[
-            pltpu.VMEM((seg_count, rows_pool, width), bf16),
+            pltpu.VMEM((seg_count, rows_pool, width // 2), bf16),
             pltpu.VMEM((tokens, width), bf16),
             pltpu.VMEM((mp_count, tokens, width), bf16),
             pltpu.VMEM((mp_count, 16, width), bf16),
-            pltpu.VMEM((mp_count, width, in_width), bf16),
-            pltpu.VMEM((D, in_width), bf16),
+            pltpu.VMEM((mp_count, width, q_width), bf16),
+            pltpu.VMEM((mp_count, width, kv_lanes), bf16),
+            pltpu.VMEM((D, q_width), bf16),
+            pltpu.VMEM((D, kv_lanes), bf16),
             pltpu.VMEM((mp_count * q_width, width), bf16),
             pltpu.VMEM((mp_count, tokens, in_width), bf16),
             pltpu.VMEM((mp_count, tokens, in_width), bf16),
@@ -416,37 +502,38 @@
             pltpu.VMEM((mp_count, 8, tokens), f32),
             pltpu.VMEM((8, tokens), f32),
             pltpu.VMEM((8, tokens), f32),
-            dma((3,)),
+            dma((4,)),
             dma((2, seg_count)),
             dma((2, mp_count)),
             dma((2, mp_count)),
             dma((2, mp_count)),
-            dma((2, mp_count)),
-            dma((2, mp_count)),
+            dma((2, 2 * mp_count)),
+            dma((2, 2 * mp_count)),
+            dma((2, 2 * mp_count)),
             dma((2, group)),
             dma((2, mp_count)),
-            dma((2, 1)),
+            dma((2, 2)),
             dma((2, seg_count)),
             dma((2, mp_count)),
             dma((2, seg_count)),
             dma((2, 1)),
         ],
         compiler_params=pltpu.CompilerParams(
-            collective_id=0, has_side_effects=True, vmem_limit_bytes=44 * 1024 * 1024
+            collective_id=0, has_side_effects=True, vmem_limit_bytes=58 * 1024 * 1024
         ),
     )(
         resp_rows.reshape(rows_pool, width),
         pick[:, None],
         code[:, None],
-        base[:, None],
         code[None, :],
         cosine,
         signed_sine,
         jnp.broadcast_to(gains[0], (16, width)),
-        w_in,
+        w_query[0, 0],
+        keyval_w,
         w_out[0, 0],
-        lift,
-        lift * head.astype(f32),
+        final_gain,
+        head,
     )
 
     def restored(row):

time: 150 us -> 130 us (0.87)
  Pallas kernels: 127 us -> 115 us
  other arithmetic: 8.04 us -> 4.08 us
  local copies, waits for them, and re-layouts: 13.5 us -> 10.7 us
    pallas_call x1, Pallas kernels: 127 us -> 115 us  [per_device(): pl.pallas_call(functools.partial(stack_kernel, mp_count, seg_count, kv_wi...]
    unnamed x13 -> x5, local copies, waits for them, and re-layouts: 6.79 us -> 1.68 us
    concatenate x1 -> x0, other arithmetic: 2.6 us -> none  [per_device(): jnp.concatenate([w_query[0, 0], keyval_w, jnp.zeros((D, kv_lanes - 2 * kv...]
where the time goes in v3:
time: 130 us
  Pallas kernels  115 us (88%)
  local copies, waits for them, and re-layouts  10.7 us (8%)
  other arithmetic  4.08 us (3%)
    pallas_call x1, Pallas kernels, per_device(): pl.pallas_call(functools.partial(stack_kernel, mp_count, seg_count, kv_wi...  115 us

profile of v3, /device:TPU:0, one launch (start us, length us, event | category | flops | bytes accessed | tf_op | source)
XLA Modules:
  0.0 130.1 jit_solution(1251304855638806762)
XLA Ops:
  0.6 0.9 reduce_window_sum.11
  1.5 0.7 broadcast_add_fusion
  2.2 0.1 convert_reduce_fusion
  2.3 0.7 mul.105
  3.0 0.1 select_reduce_fusion.1
  3.4 0.1 convert_element_type.24
  3.5 0.5 fusion
  4.1 0.8 pad_maximum_fusion
  4.9 0.8 add.85.code_col
  5.7 0.6 add.81.code_row
  6.3 0.8 add.84.pick
  7.1 1.5 %copy.35 = bf16[4096,64]{1,0:T(8,128)(2,1)S(1)} copy(bf16[4096,64]{0,1:T(8,128)(2,1)} %bitcast.25) | data formatting | bytes 1048576 | tf_op jit(solution)/shard_map/reshape;squeeze | solution.py:468
  8.7 1.2 pad.4.w_keyval
  9.9 0.6 broadcast_in_dim.5.gain
  10.5 114.6 %shard_map.112 = (bf16[128,1024]{1,0:T(8,128)(2,1)}, f32[8,256]{1,0:T(8,128)}, f32[8,256]{1,0:T(8,128)}) custom-call(bf16[256,1024]{1,0:T(8,128)(2,1)} %bitcast.26, s32[256,1]{1,0:T(8,128)} %add.84.pick, s32[256,1]{1,0:T(8,128)} %add.85.code_col, s32[1,256]{1,0:T(1,128)} %add.81.code_row, f32[256,128]{1,0:T(8,128)} %get-tuple-element.19.cosine, ...), custom_call_target="tpu_custom_call" | custom-call | tf_op jit(solution)/shard_map/pallas_call | solution.py:476
  125.1 0.7 slice_reduce_fusion.1
  125.8 0.1 reshape_squeeze.10
  125.9 0.7 slice_reduce_fusion
  126.6 0.1 reshape_squeeze.11
  126.8 0.2 select_reduce_fusion
  127.0 0.1 mul.122
  127.1 0.7 select_reduce_fusion.3
  127.8 0.7 broadcast_in_dim_reshape.2
  128.4 1.7 %copy.46 = bf16[1,4,32,1024]{3,2,1,0:T(8,128)(2,1)} copy(bf16[1,4,32,1024]{3,2,1,0:T(8,128)(2,1)} %bitcast.27) | data formatting | bytes 524288
  (20 shorter events, 0.5 us)
Async XLA Ops:
  4.9 5.0 %copy-start = (bf16[1,1,1024]{2,1,0:T(2,128)(2,1)S(1)}, bf16[1,1,1024]{2,1,0:T(2,128)(2,1)}, u32[]{:S(2)}) copy-start(bf16[1,1,1024]{2,1,0:T(2,128)(2,1)} %param.15) | copy-start | bytes 6148
  10.5 116.6 %copy-start.1 = (s32[16]{0:T(128)S(1)}, s32[16]{0:T(128)}, u32[]{:S(2)}) copy-start(s32[16]{0:T(128)} %param.11) | copy-start | bytes 196

commit v4 on v3

--- a/solution.py
+++ b/solution.py
@@ -76,6 +76,8 @@
     part_in,
     acc,
     kv_all,
+    key_rows,
+    value_rows,
     att,
     y,
     y_in,
@@ -154,9 +156,35 @@
     def rows_of(index):
         return pl.ds(pl.multiple_of(index * width, width), width)
 
-    ss_lane = q_width + 2 * kv_width
     kv_lanes = in_width - q_width
     my_columns = pl.ds(pl.multiple_of(core * half_width, half_width), half_width)
+
+    def rows_at(r):
+        return pl.ds(r * half, half)
+
+    def gain_copy(d):
+        return remote(gain, gain_all.at[me], gain_sem, d, mp=peer(d))
+
+    def shard_copy(r, d):
+        return remote(
+            x_own.at[rows_at(r), my_columns],
+            x_all.at[me, rows_at(r), my_columns],
+            half_sem,
+            r * mp_count + d,
+            mp=peer(d),
+        )
+
+    def swap_copy(r, d):
+        here = x_own.at[rows_at(r), my_columns]
+        if d > 0:
+            here = x_all.at[source_of(d), rows_at(r), my_columns]
+        return remote(here, here, swap_sem, r * mp_count + d, section=1 - core)
+
+    def part_copy(r, d):
+        mine = rows_at(r)
+        return remote(
+            part_out.at[d, mine], part_in.at[d, mine], part_sem, r * mp_count + d, mp=peer(d)
+        )
 
     @pl.when(seg == 0)
     def _():
@@ -167,11 +195,8 @@
         own_keyval = pltpu.make_async_copy(w_keyval, keyval_own, local_sem.at[2])
         own_keyval.start()
         gain_all[me] = gain[...]
-        gain_copies = [
-            remote(gain, gain_all.at[me], gain_sem, d, mp=peer(d)) for d in range(1, mp_count)
-        ]
-        for copy in gain_copies:
-            copy.start()
+        for d in range(1, mp_count):
+            gain_copy(d).start()
         row_ids = lax.broadcasted_iota(jnp.int32, (tokens, rows_pool), 1)
         chosen = [
             (pick[...] - s * rows_pool == row_ids).astype(f32).astype(bf16) for s in range(seg_count)
@@ -185,53 +210,14 @@
             for s in range(1, seg_count):
                 found += jnp.dot(chosen[s], pool[s, :, at : at + step], preferred_element_type=f32)
             x_own[:, pl.ds(pl.multiple_of(core * half_width + at, step), step)] = found.astype(bf16)
-        packed = x_own.at[:, my_columns]
-        halves = [
-            remote(packed, x_all.at[me, :, my_columns], half_sem, d, mp=peer(d))
-            for d in range(1, mp_count)
-        ]
-        for copy in halves:
-            copy.start()
-        swaps = [remote(packed, packed, swap_sem, 0, section=1 - core)]
-        swaps[0].start()
+        for r in range(2):
+            for d in range(1, mp_count):
+                shard_copy(r, d).start()
+            swap_copy(r, 0).start()
         own_query.wait()
         own_keyval.wait()
-        lane = lax.broadcasted_iota(jnp.int32, (tokens, kv_lanes), 1)
-
-        def shard(values, gains_row, index):
-            rows = values.astype(f32)
-            squares = jnp.sum(rows * rows, axis=1, keepdims=True)
-            lifted = (rows * gains_row.astype(f32)).astype(bf16)
-            at = rows_of(index)
-            acc[:, :q_width] += jnp.dot(lifted, query_own[at], preferred_element_type=f32)
-            keyval = jnp.dot(lifted, keyval_own[at], preferred_element_type=f32)
-            acc[:, q_width:] += keyval + jnp.where(lane == 2 * kv_width, squares, 0.0)
-
-        def add(d):
-            swaps[d].wait_recv()
-            if d == 0:
-                shard(x_own[...], gain[0:1], me)
-            else:
-                gain_copies[d - 1].wait_recv()
-                index = source_of(d)
-                shard(x_all[index], gain_all[index, 0:1], index)
-
-        acc[...] = jnp.zeros_like(acc)
         for d in range(1, mp_count):
-            here = x_all.at[source_of(d), :, my_columns]
-            swaps.append(remote(here, here, swap_sem, d, section=1 - core))
-        order = []
-        for d in range(1, mp_count // 2 + 1):
-            order += [d] if 2 * d == mp_count else [d, mp_count - d]
-        done = 0
-        for d in order:
-            halves[d - 1].wait_recv()
-            swaps[d].start()
-            add(done)
-            done = d
-        add(done)
-        for copy in halves + swaps + gain_copies:
-            copy.wait_send()
+            gain_copy(d).wait_recv()
 
     @pl.when(seg > 0)
     def _():
@@ -266,13 +252,48 @@
             share.wait()
         for copy in shards:
             copy.wait_send()
-        lane = lax.broadcasted_iota(jnp.int32, (half, kv_lanes), 1)
-        copies = []
-        for r in range(2):
-            mine = pl.ds(r * half, half)
-            remote(
-                y.at[mine], x_own.at[mine], next_sem, r, segment=lax.rem(seg + 1, seg_count)
-            ).wait_recv()
+
+    slot = lax.rem(me, group)
+    lane = lax.broadcasted_iota(jnp.int32, (half, kv_lanes), 1)
+    head_count = q_width // HEAD_DIM
+    att_columns = pl.ds(pl.multiple_of(me * q_width, q_width), q_width)
+    order = []
+    for d in range(1, mp_count // 2 + 1):
+        order += [d] if 2 * d == mp_count else [d, mp_count - d]
+
+    def project_in(r):
+        mine = rows_at(r)
+
+        @pl.when(seg == 0)
+        def _():
+            acc[mine] = jnp.zeros((half, in_width), f32)
+
+            def add(d):
+                swap_copy(r, d).wait_recv()
+                if d == 0:
+                    values, gains_row, index = x_own[mine], gain[0:1], me
+                else:
+                    index = source_of(d)
+                    values, gains_row = x_all[index, mine], gain_all[index, 0:1]
+                rows = values.astype(f32)
+                squares = jnp.sum(rows * rows, axis=1, keepdims=True)
+                lifted = (rows * gains_row.astype(f32)).astype(bf16)
+                at = rows_of(index)
+                acc[mine, :q_width] += jnp.dot(lifted, query_own[at], preferred_element_type=f32)
+                keyval = jnp.dot(lifted, keyval_own[at], preferred_element_type=f32)
+                acc[mine, q_width:] += keyval + jnp.where(lane == 2 * kv_width, squares, 0.0)
+
+            done = 0
+            for d in order:
+                shard_copy(r, d).wait_recv()
+                swap_copy(r, d).start()
+                add(done)
+                done = d
+            add(done)
+
+        @pl.when(seg > 0)
+        def _():
+            onward(r).wait_recv()
             rows = x_own[mine].astype(f32)
             squares = jnp.sum(rows * rows, axis=1, keepdims=True)
             upper = squares.astype(bf16).astype(f32)
@@ -290,83 +311,78 @@
                 part_out[d, mine, q_width:] = (
                     jnp.dot(lifted, keyval_part[index], preferred_element_type=f32) + extra
                 ).astype(bf16)
-                copies.append(
-                    remote(
-                        part_out.at[d, mine],
-                        part_in.at[d, mine],
-                        part_sem,
-                        r * mp_count + d,
-                        mp=index,
-                    )
-                )
-                copies[-1].start()
+                part_copy(r, d).start()
             acc[mine, :q_width] = jnp.dot(lifted, query_part[me], preferred_element_type=f32)
             acc[mine, q_width:] = (
                 jnp.dot(lifted, keyval_part[me], preferred_element_type=f32) + extra
             )
-        for r in range(2):
-            mine = pl.ds(r * half, half)
-            for d in range(1, mp_count):
-                copies[r * (mp_count - 1) + d - 1].wait_recv()
+            for d in order:
+                part_copy(r, d).wait_recv()
                 acc[mine] += part_in[d, mine].astype(f32)
-        for copy in copies:
-            copy.wait_send()
-
-    squares = acc[:, ss_lane : ss_lane + 1] + acc[:, ss_lane + 1 : ss_lane + 2]
-    scale = lax.rsqrt(squares / D + epsilon)
-    slot = lax.rem(me, group)
-    kv_all[slot] = (acc[:, q_width:] * scale).astype(bf16)
-    kv_copies = [
-        remote(
-            kv_all.at[slot], kv_all.at[slot], kv_sem, d, mp=me - slot + lax.rem(slot + d, group)
-        )
-        for d in range(1, group)
-    ]
-    for copy in kv_copies:
-        copy.start()
-    cos_here, sin_here = cosine[...], signed_sine[...]
-    head_count = q_width // HEAD_DIM
-    queries = []
-    for h in range(head_count):
-        vectors = acc[:, h * HEAD_DIM : (h + 1) * HEAD_DIM] * scale
-        queries.append(spin(vectors, cos_here, sin_here).astype(bf16))
-    codes = code_row[...]
-    visible = (codes <= code_col[...]) & (codes >= code_col[...] // T_MB * T_MB)
-    for copy in kv_copies:
-        copy.wait()
-    from_lane = lax.broadcasted_iota(jnp.int32, (kv_lanes, 2 * HEAD_DIM), 0)
-    to_lane = lax.broadcasted_iota(jnp.int32, (kv_lanes, 2 * HEAD_DIM), 1)
-    keyval = jnp.zeros((tokens, 2 * HEAD_DIM), f32)
-    for g in range(group):
-        place = jnp.where(
-            from_lane < kv_width,
-            from_lane + g * kv_width,
-            from_lane - kv_width + HEAD_DIM + g * kv_width,
-        )
-        moved = (place == to_lane) & (from_lane < 2 * kv_width)
-        keyval += jnp.dot(kv_all[g], moved.astype(f32).astype(bf16), preferred_element_type=f32)
-    key_rows = spin(keyval[:, :HEAD_DIM], cos_here, sin_here).astype(bf16)
-    value_rows = keyval[:, HEAD_DIM:].astype(bf16)
-    outs = []
-    for h in range(head_count):
-        logits = lax.dot_general(
-            queries[h], key_rows, (((1,), (1,)), ((), ())), preferred_element_type=f32
-        ) * HEAD_DIM ** (-0.5)
-        logits = jnp.where(visible, logits, -1e30)
-        expo = jnp.exp(logits - jnp.max(logits, axis=1, keepdims=True))
-        weights = (expo / jnp.sum(expo, axis=1, keepdims=True)).astype(bf16)
-        outs.append(jnp.dot(weights, value_rows, preferred_element_type=f32).astype(bf16))
-    att_columns = pl.ds(pl.multiple_of(me * q_width, q_width), q_width)
-    att[:, att_columns] = jnp.concatenate(outs, axis=1)
-    att_copies = [
-        remote(att.at[:, att_columns], att.at[:, att_columns], att_sem, d, mp=peer(d))
-        for d in range(1, mp_count)
-    ]
-    for copy in att_copies:
-        copy.start()
-    proj_copy.wait()
-    for copy in att_copies:
-        copy.wait()
+
+    def att_copy(r, d):
+        here = att.at[rows_at(r), att_columns]
+        return remote(here, here, att_sem, r * mp_count + d, mp=peer(d))
+
+    def attend(r):
+        mine = rows_at(r)
+        seen = (r + 1) * half
+        ss_at = q_width + 2 * kv_width
+        squares = acc[mine, ss_at : ss_at + 1] + acc[mine, ss_at + 1 : ss_at + 2]
+        scale = lax.rsqrt(squares / D + epsilon)
+        kv_all[slot, mine] = (acc[mine, q_width:] * scale).astype(bf16)
+        kv_copies = [
+            remote(
+                kv_all.at[slot, mine],
+                kv_all.at[slot, mine],
+                kv_sem,
+                r * group + d,
+                mp=me - slot + lax.rem(slot + d, group),
+            )
+            for d in range(1, group)
+        ]
+        for copy in kv_copies:
+            copy.start()
+        cos_here, sin_here = cosine[mine], signed_sine[mine]
+        queries = []
+        for h in range(head_count):
+            vectors = acc[mine, h * HEAD_DIM : (h + 1) * HEAD_DIM] * scale
+            queries.append(spin(vectors, cos_here, sin_here).astype(bf16))
+        codes = code_row[:, :seen]
+        own_codes = code_col[mine]
+        visible = (codes <= own_codes) & (codes >= own_codes // T_MB * T_MB)
+        from_lane = lax.broadcasted_iota(jnp.int32, (kv_lanes, 2 * HEAD_DIM), 0)
+        to_lane = lax.broadcasted_iota(jnp.int32, (kv_lanes, 2 * HEAD_DIM), 1)
+        for copy in kv_copies:
+            copy.wait()
+        keyval = jnp.zeros((half, 2 * HEAD_DIM), f32)
+        for g in range(group):
+            place = jnp.where(
+                from_lane < kv_width,
+                from_lane + g * kv_width,
+                from_lane - kv_width + HEAD_DIM + g * kv_width,
+            )
+            moved = (place == to_lane) & (from_lane < 2 * kv_width)
+            keyval += jnp.dot(
+                kv_all[g, mine], moved.astype(f32).astype(bf16), preferred_element_type=f32
+            )
+        key_rows[mine] = spin(keyval[:, :HEAD_DIM], cos_here, sin_here).astype(bf16)
+        value_rows[mine] = keyval[:, HEAD_DIM:].astype(bf16)
+        outs = []
+        for h in range(head_count):
+            logits = lax.dot_general(
+                queries[h], key_rows[:seen], (((1,), (1,)), ((), ())), preferred_element_type=f32
+            ) * HEAD_DIM ** (-0.5)
+            logits = jnp.where(visible, logits, -1e30)
+            expo = jnp.exp(logits - jnp.max(logits, axis=1, keepdims=True))
+            weights = (expo / jnp.sum(expo, axis=1, keepdims=True)).astype(bf16)
+            outs.append(
+                jnp.dot(weights, value_rows[:seen], preferred_element_type=f32).astype(bf16)
+            )
+        att[mine, att_columns] = jnp.concatenate(outs, axis=1)
+        for d in range(1, mp_count):
+            att_copy(r, d).start()
+
     step = 256
 
     def onward(r):
@@ -375,8 +391,10 @@
             y.at[mine], x_own.at[mine], next_sem, r, segment=lax.rem(seg + 1, seg_count)
         )
 
-    for r in range(2):
-        mine = pl.ds(r * half, half)
+    def project_out(r):
+        mine = rows_at(r)
+        for d in range(1, mp_count):
+            att_copy(r, d).wait()
         for at in range(0, width, step):
             projected = jnp.dot(
                 att[mine], w_proj[:, at : at + step], preferred_element_type=f32
@@ -388,6 +406,30 @@
         @pl.when(seg < last)
         def _():
             onward(r).start()
+
+    project_in(0)
+    attend(0)
+    project_in(1)
+    proj_copy.wait()
+    project_out(0)
+    attend(1)
+    project_out(1)
+
+    @pl.when(seg == 0)
+    def _():
+        for d in range(1, mp_count):
+            gain_copy(d).wait_send()
+        for r in range(2):
+            for d in range(mp_count):
+                swap_copy(r, d).wait_send()
+                if d > 0:
+                    shard_copy(r, d).wait_send()
+
+    @pl.when(seg > 0)
+    def _():
+        for r in range(2):
+            for d in range(1, mp_count):
+                part_copy(r, d).wait_send()
 
     lift = final_gain[...].astype(f32)
     lift_head = lift * head[...].astype(f32)
@@ -496,6 +538,8 @@
             pltpu.VMEM((mp_count, tokens, in_width), bf16),
             pltpu.VMEM((tokens, in_width), f32),
             pltpu.VMEM((group, tokens, kv_lanes), bf16),
+            pltpu.VMEM((tokens, HEAD_DIM), bf16),
+            pltpu.VMEM((tokens, HEAD_DIM), bf16),
             pltpu.VMEM((tokens, mp_count * q_width), bf16),
             pltpu.VMEM((tokens, width), bf16),
             pltpu.VMEM((block, width), bf16),
@@ -505,13 +549,13 @@
             dma((4,)),
             dma((2, seg_count)),
             dma((2, mp_count)),
-            dma((2, mp_count)),
-            dma((2, mp_count)),
             dma((2, 2 * mp_count)),
             dma((2, 2 * mp_count)),
             dma((2, 2 * mp_count)),
-            dma((2, group)),
-            dma((2, mp_count)),
+            dma((2, 2 * mp_count)),
+            dma((2, 2 * mp_count)),
+            dma((2, 2 * group)),
+            dma((2, 2 * mp_count)),
             dma((2, 2)),
             dma((2, seg_count)),
             dma((2, mp_count)),

time: 130 us -> 124 us (0.954)
  Pallas kernels: 115 us -> 109 us
    pallas_call x1, Pallas kernels: 115 us -> 109 us  [per_device(): pl.pallas_call(functools.partial(stack_kernel, mp_count, seg_count, kv_wi...]
where the time goes in v4:
time: 124 us
  Pallas kernels  109 us (88%)
  local copies, waits for them, and re-layouts  10.7 us (9%)
  other arithmetic  4.08 us (3%)
    pallas_call x1, Pallas kernels, per_device(): pl.pallas_call(functools.partial(stack_kernel, mp_count, seg_count, kv_wi...  109 us

profile of v4, /device:TPU:0, one launch (start us, length us, event | category | flops | bytes accessed | tf_op | source)
XLA Modules:
  0.0 124.1 jit_solution(9292122452255746927)
XLA Ops:
  0.6 0.9 reduce_window_sum.11
  1.5 0.7 broadcast_add_fusion
  2.2 0.1 convert_reduce_fusion
  2.3 0.7 mul.105
  3.0 0.1 select_reduce_fusion.1
  3.4 0.1 convert_element_type.24
  3.5 0.5 fusion
  4.1 0.8 pad_maximum_fusion
  4.9 0.8 add.85.code_col
  5.7 0.6 add.81.code_row
  6.3 0.8 add.84.pick
  7.1 1.5 %copy.35 = bf16[4096,64]{1,0:T(8,128)(2,1)S(1)} copy(bf16[4096,64]{0,1:T(8,128)(2,1)} %bitcast.25) | data formatting | bytes 1048576 | tf_op jit(solution)/shard_map/reshape;squeeze | solution.py:510
  8.7 1.2 pad.4.w_keyval
  9.9 0.6 broadcast_in_dim.5.gain
  10.5 108.6 %shard_map.112 = (bf16[128,1024]{1,0:T(8,128)(2,1)}, f32[8,256]{1,0:T(8,128)}, f32[8,256]{1,0:T(8,128)}) custom-call(bf16[256,1024]{1,0:T(8,128)(2,1)} %bitcast.26, s32[256,1]{1,0:T(8,128)} %add.84.pick, s32[256,1]{1,0:T(8,128)} %add.85.code_col, s32[1,256]{1,0:T(1,128)} %add.81.code_row, f32[256,128]{1,0:T(8,128)} %get-tuple-element.19.cosine, ...), custom_call_target="tpu_custom_call" | custom-call | tf_op jit(solution)/shard_map/pallas_call | solution.py:518
  119.1 0.7 slice_reduce_fusion.1
  119.8 0.1 reshape_squeeze.10
  119.9 0.7 slice_reduce_fusion
  120.6 0.1 reshape_squeeze.11
  120.8 0.2 select_reduce_fusion
  121.0 0.1 mul.122
  121.1 0.7 select_reduce_fusion.3
  121.8 0.7 broadcast_in_dim_reshape.2
  122.4 1.7 %copy.46 = bf16[1,4,32,1024]{3,2,1,0:T(8,128)(2,1)} copy(bf16[1,4,32,1024]{3,2,1,0:T(8,128)(2,1)} %bitcast.27) | data formatting | bytes 524288
  (20 shorter events, 0.5 us)
Async XLA Ops:
  4.9 5.0 %copy-start = (bf16[1,1,1024]{2,1,0:T(2,128)(2,1)S(1)}, bf16[1,1,1024]{2,1,0:T(2,128)(2,1)}, u32[]{:S(2)}) copy-start(bf16[1,1,1024]{2,1,0:T(2,128)(2,1)} %param.15) | copy-start | bytes 6148
  10.5 110.6 %copy-start.1 = (s32[16]{0:T(128)S(1)}, s32[16]{0:T(128)}, u32[]{:S(2)}) copy-start(s32[16]{0:T(128)} %param.11) | copy-start | bytes 196

commit v5 on v4

--- a/solution.py
+++ b/solution.py
@@ -210,9 +210,9 @@
             for s in range(1, seg_count):
                 found += jnp.dot(chosen[s], pool[s, :, at : at + step], preferred_element_type=f32)
             x_own[:, pl.ds(pl.multiple_of(core * half_width + at, step), step)] = found.astype(bf16)
+        for d in range(1, mp_count):
+            shard_copy(0, d).start()
         for r in range(2):
-            for d in range(1, mp_count):
-                shard_copy(r, d).start()
             swap_copy(r, 0).start()
         own_query.wait()
         own_keyval.wait()
@@ -287,6 +287,9 @@
             for d in order:
                 shard_copy(r, d).wait_recv()
                 swap_copy(r, d).start()
+                if r == 0 and d == order[-1]:
+                    for later in range(1, mp_count):
+                        shard_copy(1, later).start()
                 add(done)
                 done = d
             add(done)

time: 124 us -> 124 us (level)
  no operation moved by 1% of the time
where the time goes in v5:
time: 124 us
  Pallas kernels  108 us (87%)
  local copies, waits for them, and re-layouts  10.7 us (9%)
  other arithmetic  4.08 us (3%)
    pallas_call x1, Pallas kernels, per_device(): pl.pallas_call(functools.partial(stack_kernel, mp_count, seg_count, kv_wi...  108 us

profile of v5, /device:TPU:0, one launch (start us, length us, event | category | flops | bytes accessed | tf_op | source)
XLA Modules:
  0.0 123.8 jit_solution(6534214042713341635)
XLA Ops:
  0.6 0.9 reduce_window_sum.11
  1.5 0.7 broadcast_add_fusion
  2.2 0.1 convert_reduce_fusion
  2.3 0.7 mul.105
  3.0 0.1 select_reduce_fusion.1
  3.4 0.1 convert_element_type.24
  3.5 0.5 fusion
  4.1 0.8 pad_maximum_fusion
  4.9 0.8 add.85.code_col
  5.7 0.6 add.81.code_row
  6.3 0.8 add.84.pick
  7.1 1.5 %copy.35 = bf16[4096,64]{1,0:T(8,128)(2,1)S(1)} copy(bf16[4096,64]{0,1:T(8,128)(2,1)} %bitcast.25) | data formatting | bytes 1048576 | tf_op jit(solution)/shard_map/reshape;squeeze | solution.py:513
  8.7 1.2 pad.4.w_keyval
  9.9 0.6 broadcast_in_dim.5.gain
  10.5 108.3 %shard_map.112 = (bf16[128,1024]{1,0:T(8,128)(2,1)}, f32[8,256]{1,0:T(8,128)}, f32[8,256]{1,0:T(8,128)}) custom-call(bf16[256,1024]{1,0:T(8,128)(2,1)} %bitcast.26, s32[256,1]{1,0:T(8,128)} %add.84.pick, s32[256,1]{1,0:T(8,128)} %add.85.code_col, s32[1,256]{1,0:T(1,128)} %add.81.code_row, f32[256,128]{1,0:T(8,128)} %get-tuple-element.19.cosine, ...), custom_call_target="tpu_custom_call" | custom-call | tf_op jit(solution)/shard_map/pallas_call | solution.py:521
  118.8 0.7 slice_reduce_fusion.1
  119.6 0.1 reshape_squeeze.10
  119.6 0.7 slice_reduce_fusion
  120.4 0.1 reshape_squeeze.11
  120.5 0.2 select_reduce_fusion
  120.7 0.1 mul.122
  120.8 0.7 select_reduce_fusion.3
  121.5 0.7 broadcast_in_dim_reshape.2
  122.2 1.7 %copy.46 = bf16[1,4,32,1024]{3,2,1,0:T(8,128)(2,1)} copy(bf16[1,4,32,1024]{3,2,1,0:T(8,128)(2,1)} %bitcast.27) | data formatting | bytes 524288
  (20 shorter events, 0.5 us)
Async XLA Ops:
  4.9 5.0 %copy-start = (bf16[1,1,1024]{2,1,0:T(2,128)(2,1)S(1)}, bf16[1,1,1024]{2,1,0:T(2,128)(2,1)}, u32[]{:S(2)}) copy-start(bf16[1,1,1024]{2,1,0:T(2,128)(2,1)} %param.15) | copy-start | bytes 6148
  10.5 110.3 %copy-start.1 = (s32[16]{0:T(128)S(1)}, s32[16]{0:T(128)}, u32[]{:S(2)}) copy-start(s32[16]{0:T(128)} %param.11) | copy-start | bytes 196
